TPU v7x, 128 devices: a whole 4x4x4 slice. The times are simulated.
128 devices in a mesh: gx: 4 (over z), gz: 16 (over y, x_hi, core), sa: 2 (over x_lo).
Axes of the slice: x: 4 (x_hi: 2, x_lo: 2; x = x_hi * 2 + x_lo), y: 4, z: 4, core: 2. Of those that a mesh axis runs over, the one named last changes fastest.
Arguments:
- forcing: float32 [3, 8, 128, 128, 256], P(None, 'sa', 'gx', 'gz'), may hold values from -60 to 60
- velocity: float32 [256], replicated, may hold values from 0.3 to 1.2
- wall_solve: float32 [256, 256], replicated, may hold values from -1 to 1.7
Outputs:
- basis: float32 [3, 8, 128, 128, 256], P(None, 'sa', 'gx', 'gz')
- factor: float32 [8, 8], replicated
All inputs are finite; a program needn't handle non-finite values.
Results may differ from a plain program's by a relative error of at most 0.00015.
Values sent between devices are 32-bit elements; how exact they have to be, the bound alone decides.
A program may use at most 64 MiB of HBM per device.

v0:
```python
import jax
import jax.numpy as jnp
from jax import lax
from jax.sharding import PartitionSpec as P

step_length = 0.4
viscosity = 0.2


def extended(cells, sides, width):
    for axis, dim in sides:
        count = lax.axis_size(axis)
        head = lax.slice_in_dim(cells, 0, width, axis=dim)
        tail = lax.slice_in_dim(cells, cells.shape[dim] - width, cells.shape[dim], axis=dim)
        cells = jnp.concatenate(
            [
                lax.ppermute(tail, axis, [(i, (i + 1) % count) for i in range(count)]),
                cells,
                lax.ppermute(head, axis, [((i + 1) % count, i) for i in range(count)]),
            ],
            axis=dim,
        )
    return cells


def shear_of(velocity):
    inner = (velocity[2:] - velocity[:-2]) * 0.5
    return jnp.concatenate([velocity[1:2] - velocity[0:1], inner, velocity[-1:] - velocity[-2:-1]])


def upper_factor(gram):
    order_size = gram.shape[0]
    column_ids = jnp.arange(order_size)
    row_list = []
    for pivot_index in range(order_size):
        current_row = gram[pivot_index]
        for other_index in range(pivot_index):
            current_row = current_row - row_list[other_index][pivot_index] * row_list[other_index]
        current_row = jnp.where(
            column_ids >= pivot_index, current_row, jnp.zeros_like(current_row)
        ) / jnp.sqrt(current_row[pivot_index])
        row_list.append(current_row)
    return jnp.stack(row_list)


def upper_inverse(factor):
    order_size = factor.shape[0]
    identity_rows = jnp.eye(order_size, dtype=factor.dtype)
    row_list = [None] * order_size
    for pivot_index in range(order_size - 1, -1, -1):
        current_row = identity_rows[pivot_index]
        for other_index in range(pivot_index + 1, order_size):
            current_row = current_row - factor[pivot_index, other_index] * row_list[other_index]
        row_list[pivot_index] = current_row / factor[pivot_index, pivot_index]
    return jnp.stack(row_list)


def stencil(padded, velocity, shear_rate, adjoint):
    center = padded[:, :, 1:-1, 1:-1]
    east_side = padded[:, :, 2:, 1:-1]
    west_side = padded[:, :, :-2, 1:-1]
    north_side = padded[:, :, 1:-1, 2:]
    south_side = padded[:, :, 1:-1, :-2]
    direction = 1.0 if adjoint else -1.0
    change = direction * velocity * (east_side - west_side) * 0.5 + viscosity * (
        east_side + west_side + north_side + south_side - 4.0 * center
    )
    if adjoint:
        change = change.at[1].add(-shear_rate * center[0])
    else:
        change = change.at[0].add(-shear_rate * center[1])
    return (center, change)


def wall_apply(field, wall_solve):
    return jnp.matmul(field, wall_solve, precision=lax.Precision.HIGHEST)


def wall_adjoint(field, wall_solve):
    return jnp.matmul(field, wall_solve.T, precision=lax.Precision.HIGHEST)


def near_faces(field):
    return extended(field, (("gx", 2), ("gz", 3)), 1)


def shards(forcing, velocity, wall_solve):
    shear_rate = shear_of(velocity)
    columns = forcing.shape[1]
    entries = (
        3
        * forcing.shape[2]
        * lax.axis_size("gx")
        * forcing.shape[3]
        * lax.axis_size("gz")
        * forcing.shape[4]
    )
    current = forcing
    for repeat in range(2):
        center, change = stencil(near_faces(current), velocity, shear_rate, False)
        current = wall_apply(center + step_length * (change + forcing), wall_solve)
    partial_value = jnp.sum(current * current, axis=(0, 2, 3, 4))
    totals = lax.psum(partial_value, ("gx", "gz"))
    scales = jnp.sqrt(totals / entries + 1e-06)
    response = current / scales[None, :, None, None, None]
    current = response
    for repeat in range(2):
        solved = wall_adjoint(current, wall_solve)
        center, change = stencil(near_faces(solved), velocity, shear_rate, True)
        current = center + step_length * change + step_length * response
    gathered = lax.all_gather(current, "sa", axis=1, tiled=True)
    half_rows = gathered.shape[4] // lax.axis_size("sa")
    row_block = lax.dynamic_slice_in_dim(gathered, lax.axis_index("sa") * half_rows, half_rows, 4)
    gram_local = jnp.einsum(
        "cixzy,cjxzy->ij", row_block, row_block, precision=lax.Precision.HIGHEST
    )
    gram = lax.psum(gram_local, ("gx", "gz", "sa")) / entries
    factor = upper_factor(gram)
    inverse = upper_inverse(factor)
    own_coef = lax.dynamic_slice_in_dim(inverse, lax.axis_index("sa") * columns, columns, 1)
    basis_own = jnp.einsum("cixzy,ij->cjxzy", gathered, own_coef, precision=lax.Precision.HIGHEST)
    return (basis_own, factor)


def solution(mesh):
    return jax.shard_map(
        shards,
        mesh=mesh,
        in_specs=(P(None, "sa", "gx", "gz", None), P(), P()),
        out_specs=(P(None, "sa", "gx", "gz", None), P()),
        check_vma=False,
    )
```

profile of v0, /device:TPU:1, one launch (start us, length us, event | category | flops | bytes accessed | tf_op | source)
XLA Modules:
  0.0 537.0 jit_solution(2911002722180236173)
XLA Ops:
  7.2 1.0 fusion.100
  8.2 2.5 collective-permute-start.1
  10.8 2.2 collective-permute-start
  13.0 0.8 subtract_multiply_fusion
  13.8 1.6 collective-permute-done.1
  15.4 2.3 constant_dynamic-update-slice_fusion.1
  18.2 1.3 collective-permute-start.2
  19.5 2.7 collective-permute-start.3
  22.8 1.4 maximum_negate_fusion
  24.2 5.4 collective-permute-done.2
  29.8 2.2 fusion.20
  32.4 2.8 fusion.32
  35.2 2.3 collective-permute-start.4
  37.5 1.6 collective-permute-done.4
  39.1 3.0 collective-permute-done.5
  42.7 6.5 %collective-permute-start.6 = (f32[3,4,34,1,256]{4,3,2,1,0:T(1,128)S(1)}, f32[3,4,34,1,256]{4,3,2,1,0:T(1,128)S(1)}, u32[]{:S(2)}, u32[]{:S(2)}) collective-permute-start(f32[3,4,34,1,256]{4,3,2,1,0:T(1,128)S(1)} %get-tuple-element.71), channel_id=1, source_target_pairs={{2,0},{4,2},{6,4},{8,6},{10,8},{12,10},{14,12},{16,14},{18,16},{20... | collective-permute-start | bytes 1253384 | tf_op jit(solution)/shard_map/ppermute | solution.py:19
  49.5 6.3 %collective-permute-done.6 = f32[3,4,34,1,256]{4,3,2,1,0:T(1,128)S(1)} collective-permute-done((f32[3,4,34,1,256]{4,3,2,1,0:T(1,128)S(1)}, f32[3,4,34,1,256]{4,3,2,1,0:T(1,128)S(1)}, u32[]{:S(2)}, u32[]{:S(2)}) %collective-permute-start.6) | collective-permute-done | bytes 417824 | tf_op jit(solution)/shard_map/ppermute | solution.py:19
  55.8 1.9 collective-permute-done.7
  57.7 2.4 fusion.15
  60.3 2.8 multiply_reduce_fusion
  63.2 166.2 %psum.14 = f32[4]{0:T(128)S(1)} all-reduce(f32[4]{0:T(128)S(1)} %get-tuple-element.140), channel_id=1, replica_groups=mesh['gx'=4,'gz'=16,'sa'=2] {'gx','gz'}, use_global_device_ids=true, to_apply=%region_1.0 | all-reduce | flops 4 | bytes 32 | tf_op jit(solution)/shard_map/psum | solution.py:103
  229.4 2.8 fusion.54
  232.3 1.5 collective-permute-start.9
  233.8 2.0 collective-permute-done.8
  235.8 1.3 collective-permute-done.9
  237.6 4.1 collective-permute-start.10
  242.2 5.2 collective-permute-done.10
  247.5 3.9 collective-permute-done.11
  251.4 2.4 fusion.10
  254.0 3.1 fusion.24
  257.2 1.5 collective-permute-start.13
  258.7 2.0 collective-permute-done.12
  260.7 1.3 collective-permute-done.13
  262.5 3.3 collective-permute-start.14
  265.8 2.2 collective-permute-start.15
  268.0 10.2 %collective-permute-done.14 = f32[3,4,34,1,256]{4,3,2,1,0:T(1,128)S(1)} collective-permute-done((f32[3,4,34,1,256]{4,3,2,1,0:T(1,128)S(1)}, f32[3,4,34,1,256]{4,3,2,1,0:T(1,128)S(1)}, u32[]{:S(2)}, u32[]{:S(2)}) %collective-permute-start.14) | collective-permute-done | bytes 417824 | tf_op jit(solution)/shard_map/ppermute | solution.py:19
  278.2 2.4 fusion.5
  280.9 2.6 add_add_fusion
  283.5 81.8 %all-gather.2.cloned.1.call-done = f32[3,8,32,8,256]{4,3,2,1,0:T(8,128)} async-done(((f32[3,4,32,8,256]{4,3,2,1,0:T(8,128)}), f32[3,8,32,8,256]{4,3,2,1,0:T(8,128)}) %all-gather.2.cloned.1.call-update) | async-done | bytes 6291472 | tf_op jit(solution)/shard_map/all_gather | solution.py:111
  365.3 2.1 constant_dynamic-slice_fusion
  367.4 7.5 %fusion.43 = f32[8,8]{1,0:T(8,128)S(1)} fusion(f32[3,8,32,8,128]{4,3,2,1,0:T(8,128)S(1)} %constant_dynamic-slice_fusion), kind=kOutput, calls=%fused_computation.72 | convolution fusion | flops 75497472 | bytes 3145984 | tf_op jit(solution)/shard_map/cixzy,cjxzy->ij/dot_general | solution.py:114
  374.9 66.0 %psum.15 = f32[8,8]{1,0:T(8,128)S(1)} all-reduce(f32[8,8]{1,0:T(8,128)S(1)} %fusion.43), channel_id=1, replica_groups=mesh['gx'=4,'gz'=16,'sa'=2] {'gx','gz','sa'}, use_global_device_ids=true, to_apply=%region_2.0 | all-reduce | flops 64 | bytes 512 | tf_op jit(solution)/shard_map/psum | solution.py:117
  442.1 0.7 fusion.112
  442.8 0.7 multiply_subtract_fusion.8
  444.6 0.7 fusion.107
  445.3 1.3 bitcast_subtract_fusion.5
  446.6 0.7 slice.588
  448.0 0.7 fusion.108
  448.7 1.9 fusion.86
  451.9 0.7 fusion.109
  452.5 2.5 fusion.85
  456.3 0.7 fusion.110
  457.0 3.1 fusion.83
  461.5 0.7 fusion.111
  462.1 3.7 multiply_subtract_fusion.2
  465.9 0.7 slice.622
  467.8 4.4 multiply_subtract_fusion
  473.6 17.0 %fusion.73 = (f32[1,8]{1,0:T(1,128)S(1)}, f32[1,8]{1,0:T(1,128)S(1)}, f32[1,8]{1,0:T(1,128)S(1)}, f32[1,8]{1,0:T(1,128)S(1)}, f32[1,8]{1,0:T(1,128)S(1)}, /*index=5*/f32[1,8]{1,0:T(1,128)S(1)}, f32[1,8]{1,0:T(1,128)S(1)}) fusion(f32[]{:T(128)} %bitcast.52, f32[]{:T(128)} %bitcast.50, f32[]{:T(128)} %bitcast.49, f32[]{:T(128)} %bitcast.48, f32[]{:T(128)} %bitcast.47, ...), kind=kLoop, calls=%fused_computation.134 | loop fusion | flops 608 | bytes 620 | tf_op jit(solution)/shard_map/div | solution.py:39
  490.6 0.7 fusion.101
  491.2 0.7 fusion.103
  491.9 0.7 fusion.105
  493.8 22.6 %subtract_divide_fusion = (f32[1,8]{1,0:T(1,128)S(1)}, f32[1,8]{1,0:T(1,128)S(1)}, f32[1,8]{1,0:T(1,128)S(1)}, f32[1,8]{1,0:T(1,128)S(1)}, f32[1,8]{1,0:T(1,128)...) fusion(f32[8,8]{1,0:T(8,128)S(1)} %fusion.60, f32[]{:T(128)} %bitcast.75, f32[]{:T(128)} %bitcast.44, ...), kind=kLoop, calls=%fused_computation.154 | loop fusion | flops 512 | bytes 656 | tf_op jit(solution)/shard_map/div | solution.py:54
  516.5 11.2 %fusion.37 = f32[3,4,32,8,256]{4,1,3,2,0:T(4,128)S(1)} fusion(f32[3,8,32,8,256]{4,3,2,1,0:T(8,128)} %all-gather.2.cloned.1.call-done, f32[8,8]{1,0:T(8,128)S(1)} %stack.4, s32[]{:T(128)S(6)} %select_n.83), kind=kOutput, calls=%fused_computation.67 | convolution fusion | flops 75497472 | bytes 9437444 | tf_op jit(solution)/shard_map/cixzy,ij->cjxzy/dot_general | solution.py:121
  527.8 2.2 copy.9
  (51 shorter events, 10.6 us)
Async XLA Ops:
  7.2 25.2 %copy-start = (f32[256,256]{1,0:T(8,128)S(1)}, f32[256,256]{1,0:T(8,128)}, u32[]{:S(2)}) copy-start(f32[256,256]{1,0:T(8,128)} %param.13) | copy-start | bytes 786436
  7.2 358.1 %all-gather.2.cloned.1.call-start = ((), (), s32[]{:S(2)}) async-start(), calls=%async_computation | async-start | bytes 9437184 | tf_op jit(solution)/shard_map/all_gather | solution.py:111
  8.2 7.2 %collective-permute-start.1 = (f32[3,4,1,8,256]{4,3,2,1,0:T(8,128)S(1)}, f32[3,4,1,8,256]{4,3,2,1,0:T(8,128)S(1)}, u32[]{:S(2)}, u32[]{:S(2)}) collective-permute-start(f32[3,4,1,8,256]{4,3,2,1,0:T(8,128)S(1)} %get-tuple-element.82), channel_id=1, source_target_pairs={{0,32},{32,64},{64,96},{96,0},{1,33},{33,65},{65,97},{97,1},{2,34}... | collective-permute-start | bytes 294920 | tf_op jit(solution)/shard_map/ppermute | solution.py:17
  10.8 7.0 %collective-permute-start = (f32[3,4,1,8,256]{4,3,2,1,0:T(8,128)S(1)}, f32[3,4,1,8,256]{4,3,2,1,0:T(8,128)S(1)}, u32[]{:S(2)}, u32[]{:S(2)}) collective-permute-start(f32[3,4,1,8,256]{4,3,2,1,0:T(8,128)S(1)} %get-tuple-element.81), channel_id=1, source_target_pairs={{32,0},{64,32},{96,64},{0,96},{33,1},{65,33},{97,65},{1,97},{34,2}... | collective-permute-start | bytes 294920 | tf_op jit(solution)/shard_map/ppermute | solution.py:19
  15.4 6.9 %copy-start.2 = (f32[256]{0:T(256)S(1)}, f32[256]{0:T(256)}, u32[]{:S(2)}) copy-start(f32[256]{0:T(256)} %param.12) | copy-start | bytes 3076
  15.4 14.4 %copy-start.1 = (f32[3,4,32,8,256]{4,3,2,1,0:T(8,128)S(1)}, f32[3,4,32,8,256]{4,3,2,1,0:T(8,128)}, u32[]{:S(2)}) copy-start(f32[3,4,32,8,256]{4,3,2,1,0:T(8,128)} %param.11) | copy-start | bytes 9437188
  18.2 11.3 %collective-permute-start.2 = (f32[3,4,34,1,256]{4,3,2,1,0:T(1,128)S(1)}, f32[3,4,34,1,256]{4,3,2,1,0:T(1,128)S(1)}, u32[]{:S(2)}, u32[]{:S(2)}) collective-permute-start(f32[3,4,34,1,256]{4,3,2,1,0:T(1,128)S(1)} %get-tuple-element.73), channel_id=1, source_target_pairs={{2,0},{4,2},{6,4},{8,6},{10,8},{12,10},{14,12},{16,14},{18,16},{20... | collective-permute-start | bytes 1253384 | tf_op jit(solution)/shard_map/ppermute | solution.py:19
  19.5 10.3 %collective-permute-start.3 = (f32[3,4,34,1,256]{4,3,2,1,0:T(1,128)S(1)}, f32[3,4,34,1,256]{4,3,2,1,0:T(1,128)S(1)}, u32[]{:S(2)}, u32[]{:S(2)}) collective-permute-start(f32[3,4,34,1,256]{4,3,2,1,0:T(1,128)S(1)} %get-tuple-element.74), channel_id=1, source_target_pairs={{0,2},{2,4},{4,6},{6,8},{8,10},{10,12},{12,14},{14,16},{16,18},{18... | collective-permute-start | bytes 1253384 | tf_op jit(solution)/shard_map/ppermute | solution.py:17
  35.2 3.9 collective-permute-start.4
  37.5 4.7 collective-permute-start.5
  42.7 13.1 %collective-permute-start.6 = (f32[3,4,34,1,256]{4,3,2,1,0:T(1,128)S(1)}, f32[3,4,34,1,256]{4,3,2,1,0:T(1,128)S(1)}, u32[]{:S(2)}, u32[]{:S(2)}) collective-permute-start(f32[3,4,34,1,256]{4,3,2,1,0:T(1,128)S(1)} %get-tuple-element.71), channel_id=1, source_target_pairs={{2,0},{4,2},{6,4},{8,6},{10,8},{12,10},{14,12},{16,14},{18,16},{20... | collective-permute-start | bytes 1253384 | tf_op jit(solution)/shard_map/ppermute | solution.py:19
  49.2 8.5 %collective-permute-start.7 = (f32[3,4,34,1,256]{4,3,2,1,0:T(1,128)S(1)}, f32[3,4,34,1,256]{4,3,2,1,0:T(1,128)S(1)}, u32[]{:S(2)}, u32[]{:S(2)}) collective-permute-start(f32[3,4,34,1,256]{4,3,2,1,0:T(1,128)S(1)} %get-tuple-element.72), channel_id=1, source_target_pairs={{0,2},{2,4},{4,6},{6,8},{8,10},{10,12},{12,14},{14,16},{16,18},{18... | collective-permute-start | bytes 1253384 | tf_op jit(solution)/shard_map/ppermute | solution.py:17
  232.2 3.5 collective-permute-start.8
  232.3 4.7 collective-permute-start.9
  237.6 9.9 %collective-permute-start.10 = (f32[3,4,34,1,256]{4,3,2,1,0:T(1,128)S(1)}, f32[3,4,34,1,256]{4,3,2,1,0:T(1,128)S(1)}, u32[]{:S(2)}, u32[]{:S(2)}) collective-permute-start(f32[3,4,34,1,256]{4,3,2,1,0:T(1,128)S(1)} %get-tuple-element.69), channel_id=1, source_target_pairs={{2,0},{4,2},{6,4},{8,6},{10,8},{12,10},{14,12},{16,14},{18,16},{20... | collective-permute-start | bytes 1253384 | tf_op jit(solution)/shard_map/ppermute | solution.py:19
  241.7 9.6 %collective-permute-start.11 = (f32[3,4,34,1,256]{4,3,2,1,0:T(1,128)S(1)}, f32[3,4,34,1,256]{4,3,2,1,0:T(1,128)S(1)}, u32[]{:S(2)}, u32[]{:S(2)}) collective-permute-start(f32[3,4,34,1,256]{4,3,2,1,0:T(1,128)S(1)} %get-tuple-element.70), channel_id=1, source_target_pairs={{0,2},{2,4},{4,6},{6,8},{8,10},{10,12},{12,14},{14,16},{16,18},{18... | collective-permute-start | bytes 1253384 | tf_op jit(solution)/shard_map/ppermute | solution.py:17
  257.2 3.5 collective-permute-start.12
  257.2 4.7 collective-permute-start.13
  262.5 15.7 %collective-permute-start.14 = (f32[3,4,34,1,256]{4,3,2,1,0:T(1,128)S(1)}, f32[3,4,34,1,256]{4,3,2,1,0:T(1,128)S(1)}, u32[]{:S(2)}, u32[]{:S(2)}) collective-permute-start(f32[3,4,34,1,256]{4,3,2,1,0:T(1,128)S(1)} %get-tuple-element.67), channel_id=1, source_target_pairs={{2,0},{4,2},{6,4},{8,6},{10,8},{12,10},{14,12},{16,14},{18,16},{20... | collective-permute-start | bytes 1253384 | tf_op jit(solution)/shard_map/ppermute | solution.py:19
  265.8 12.4 %collective-permute-start.15 = (f32[3,4,34,1,256]{4,3,2,1,0:T(1,128)S(1)}, f32[3,4,34,1,256]{4,3,2,1,0:T(1,128)S(1)}, u32[]{:S(2)}, u32[]{:S(2)}) collective-permute-start(f32[3,4,34,1,256]{4,3,2,1,0:T(1,128)S(1)} %get-tuple-element.68), channel_id=1, source_target_pairs={{0,2},{2,4},{4,6},{6,8},{8,10},{10,12},{12,14},{14,16},{16,18},{18... | collective-permute-start | bytes 1253384 | tf_op jit(solution)/shard_map/ppermute | solution.py:17
Sparse Core Ops, SparseCore 0:
  283.6 81.6 all-gather.1
where the time goes:
time: 545 us; the launch traced here: 537 us
  blocking collectives  232 us (43%)
  waiting for transfers between devices  128 us (23%)
  other arithmetic  74.8 us (14%)
  starting transfers between devices  31 us (6%)
  matrix products  30.3 us (6%)
  local copies, waits for them, and re-layouts  20.9 us (4%)
  between operations  20 us (4%)
    psum x1, blocking collectives, shards(): totals = lax.psum(partial_value, ('gx', 'gz'))  166 us
    all_gather x1, waiting for transfers between devices, shards(): gathered = lax.all_gather(current, 'sa', axis=1, tiled=True)  81.8 us
    psum x1, blocking collectives, shards(): gram = lax.psum(gram_local, ('gx', 'gz', 'sa')) / entries  66 us
    ppermute x8, waiting for transfers between devices, extended(): lax.ppermute(head, axis, [((i + 1) % count, i) for i in range(count)])  32.8 us
    div x1, other arithmetic, upper_inverse(): row_list[pivot_index] = current_row / factor[pivot_index, pivot_index]  22.6 us
    ppermute x8, starting transfers between devices, extended(): lax.ppermute(head, axis, [((i + 1) % count, i) for i in range(count)])  19.8 us
    sub x7, other arithmetic, upper_factor(): current_row - row_list[other_index][pivot_index] * row_list[other_index]  17.7 us
    div x8, other arithmetic, upper_factor(): jnp.where(column_ids >= pivot_index, current_row, jnp.zeros_like(current_...  17 us
  transfers between devices with their start and end apart: 17, of which 15 were waited for; matrix products, arithmetic and copies ran while one was open for 1% of the time, Pallas kernels for 0%

commit v1 on v0

v1 whole, which is shorter than its diff:
```python
import functools

import jax
import jax.numpy as jnp
from jax import lax
from jax.experimental import pallas as pl
from jax.experimental.pallas import tpu as pltpu
from jax.sharding import PartitionSpec as P

MESH = pl.DeviceIdType.MESH
step_length = 0.4
viscosity = 0.2
GROUPS = ((2, 1, 16), (0, 2, 8))
BLOCKS = 4
CELLS = 32
NY = 256
ROWS = 512


def kernel(
    entries,
    forcing,
    velocity,
    wall,
    basis,
    factor_out,
    field0,
    field1,
    field2,
    field3,
    held,
    sketch,
    other,
    edge_out,
    edge_in,
    lhs,
    solve,
    solve_t,
    drift_row,
    shear_row,
    squares,
    local_gram,
    row_sums,
    y_sums,
    z_sums,
    splats,
    coefs,
    load_sem,
    send_sem,
    recv_sem,
    sketch_send,
    sketch_recv,
    sum_send,
    sum_recv,
    store_sem,
):
    gx, gz, sa = lax.axis_index("gx"), lax.axis_index("gz"), lax.axis_index("sa")
    in_row, y = lax.rem(gz, 4), lax.div(gz, 4)
    rank = in_row * 2 + sa

    def row_peer(offset):
        other_rank = lax.rem(rank + offset, 8)
        return (gx, y * 4 + lax.div(other_rank, 2), lax.rem(other_rank, 2))

    def y_peer(offset):
        return (gx, lax.rem(y + offset, 4) * 4 + in_row, sa)

    def z_peer(offset):
        return (lax.rem(gx + offset, 4), gz, sa)

    def gz_peer(offset):
        return (gx, lax.rem(gz + offset + 16, 16), sa)

    def loads():
        return [
            pltpu.make_async_copy(
                forcing.at[pl.ds(c0, nc)],
                field0.at[pl.ds(c0, nc), :, pl.ds(1, CELLS)],
                load_sem.at[g],
            )
            for g, (c0, nc, _) in enumerate(GROUPS)
        ]

    for copy in loads():
        copy.start()
    barrier = pltpu.get_barrier_semaphore()
    peers = [row_peer(d) for d in range(1, 8)]
    peers += [y_peer(d) for d in range(1, 4)] + [z_peer(d) for d in range(1, 4)]
    peers += [gz_peer(1), gz_peer(-1)]
    for peer in peers:
        pl.semaphore_signal(barrier, inc=1, device_id=peer, device_id_type=MESH)

    row = velocity[...]
    lane = lax.broadcasted_iota(jnp.int32, (1, NY), 1)
    after = pltpu.roll(row, NY - 1, 1)
    before = pltpu.roll(row, 1, 1)
    shear = jnp.where(
        lane == 0, after - row, jnp.where(lane == NY - 1, row - before, (after - before) * 0.5)
    )
    drift_row[...] = row * (0.5 * step_length)
    shear_row[...] = shear * step_length

    def split_into(target, value):
        high = value.astype(jnp.bfloat16)
        low = (value - high.astype(jnp.float32)).astype(jnp.bfloat16)
        target[pl.ds(0, NY), :] = high
        target[pl.ds(NY, NY), :] = high
        target[pl.ds(2 * NY, NY), :] = low

    split_into(solve, wall[...])
    split_into(solve_t, wall[...].T)
    squares[...] = jnp.zeros_like(squares)

    def split_rows(start, value):
        rows = value.shape[0] * value.shape[1]
        flat = value.reshape(rows, NY)
        high = flat.astype(jnp.bfloat16)
        low = (flat - high.astype(jnp.float32)).astype(jnp.bfloat16)
        lhs[pl.ds(start, rows), pl.ds(0, NY)] = high
        lhs[pl.ds(start, rows), pl.ds(NY, NY)] = low
        lhs[pl.ds(start, rows), pl.ds(2 * NY, NY)] = high

    def product(weights):
        return jnp.dot(lhs[...], weights[...], preferred_element_type=jnp.float32)

    def halo_copies(e, g, field):
        c0, nc, _ = GROUPS[g]
        part = pl.ds(c0, nc)

        def remote(k, src, dst, device):
            return pltpu.make_async_remote_copy(
                src_ref=src,
                dst_ref=dst,
                send_sem=send_sem.at[e, g, k],
                recv_sem=recv_sem.at[e, g, k],
                device_id=device,
                device_id_type=MESH,
            )

        return [
            remote(0, edge_out.at[e, 0, part], edge_in.at[e, 1, part], gz_peer(1)),
            remote(1, edge_out.at[e, 1, part], edge_in.at[e, 0, part], gz_peer(-1)),
            remote(2, field.at[part, :, CELLS], field.at[part, :, 0], z_peer(1)),
            remote(3, field.at[part, :, 1], field.at[part, :, CELLS + 1], z_peer(3)),
        ]

    def put_edges(e, c, b, cells, value):
        edge_out[e, 0, c, b, cells] = value[:, 7:8, :]
        edge_out[e, 1, c, b, cells] = value[:, 0:1, :]

    def stepped(e, g, field, extra, adjoint, x0):
        c0, nc, width = GROUPS[g]
        drift = drift_row[...].reshape(1, 1, NY)
        shear = shear_row[...].reshape(1, 1, NY)
        if adjoint:
            drift = -drift
        level = lax.broadcasted_iota(jnp.int32, (width, 8, NY), 1)
        out = {}
        for b in range(BLOCKS):
            centers = [field[c, b, pl.ds(x0 + 1, width)] for c in range(c0, c0 + nc)]
            for i in range(nc):
                c = c0 + i
                center = centers[i]
                east = field[c, b, pl.ds(x0 + 2, width)]
                west = field[c, b, pl.ds(x0, width)]
                north = jnp.where(
                    level == 7, edge_in[e, 0, c, b, pl.ds(x0, width)], pltpu.roll(center, 7, 1)
                )
                south = jnp.where(
                    level == 0, edge_in[e, 1, c, b, pl.ds(x0, width)], pltpu.roll(center, 1, 1)
                )
                value = (step_length * viscosity) * ((east + west) + (north + south))
                value = value + drift * (west - east)
                if extra is None:
                    value = value + (1.0 - 4.0 * step_length * viscosity + step_length) * center
                else:
                    value = value + (1.0 - 4.0 * step_length * viscosity) * center
                    value = value + step_length * extra(c, b, x0, width)
                if nc == 2 and i == (1 if adjoint else 0):
                    value = value - shear * centers[1 - i]
                out[i, b] = value
        return out

    def passes(g, body):
        width = GROUPS[g][2]

        def one(i, carry):
            body(pl.multiple_of(i * width, width))
            return carry

        lax.fori_loop(0, CELLS // width, one, 0)

    def run_group(g, body):
        c0, nc, width = GROUPS[g]
        tile = width * 8

        def step(x0):
            body(
                x0,
                lambda values: [
                    split_rows((i * BLOCKS + b) * tile, values[i, b])
                    for i in range(nc)
                    for b in range(BLOCKS)
                ],
                lambda weights: {
                    (i, b): value
                    for prod in [product(weights)]
                    for i in range(nc)
                    for b in range(BLOCKS)
                    for value in [
                        prod[(i * BLOCKS + b) * tile : (i * BLOCKS + b + 1) * tile].reshape(
                            width, 8, NY
                        )
                    ]
                },
            )

        passes(g, step)

    def put(e, g, field, values, x0):
        c0, nc, width = GROUPS[g]
        for i in range(nc):
            for b in range(BLOCKS):
                field[c0 + i, b, pl.ds(x0 + 1, width)] = values[i, b]
                put_edges(e, c0 + i, b, pl.ds(x0, width), values[i, b])

    for g, (c0, nc, width) in enumerate(GROUPS):
        loads()[g].wait()

        def edges(x0, c0=c0, nc=nc, width=width):
            for c in range(c0, c0 + nc):
                for b in range(BLOCKS):
                    put_edges(0, c, b, pl.ds(x0, width), field0[c, b, pl.ds(x0 + 1, width)])

        passes(g, edges)
        if g == 0:
            pl.semaphore_wait(barrier, len(peers))
        for copy in halo_copies(0, g, field0):
            copy.start()

    def arrived(e, g, field):
        for copy in halo_copies(e, g, field):
            copy.wait_recv()

    def send(e, g, field):
        for copy in halo_copies(e, g, field):
            copy.start()

    def forcing_at(c, b, x0, width):
        return field0[c, b, pl.ds(x0 + 1, width)]

    def held_at(c, b, x0, width):
        return held[c, b, pl.ds(x0, width)]

    for g in range(2):
        arrived(0, g, field0)

        def first(x0, spread, solved, g=g):
            spread(stepped(0, g, field0, None, False, x0))
            put(1, g, field1, solved(solve), x0)

        run_group(g, first)
        send(1, g, field1)

    for g in range(2):
        arrived(1, g, field1)

        def second(x0, spread, solved, g=g):
            c0, nc, width = GROUPS[g]
            spread(stepped(1, g, field1, forcing_at, False, x0))
            values = solved(solve)
            for b in range(BLOCKS):
                total = squares[b]
                for i in range(nc):
                    value = values[i, b]
                    held[c0 + i, b, pl.ds(x0, width)] = value
                    total = total + jnp.sum(value * value, axis=0)
                squares[b] = total
            spread(values)
            put(2, g, field2, solved(solve_t), x0)

        run_group(g, second)
        send(2, g, field2)

    for g in range(2):
        arrived(2, g, field2)

        def third(x0, spread, solved, g=g):
            spread(stepped(2, g, field2, held_at, True, x0))
            put(3, g, field3, solved(solve_t), x0)

        run_group(g, third)
        send(3, g, field3)

    def sketch_copy(c):
        return pltpu.make_async_remote_copy(
            src_ref=sketch.at[c],
            dst_ref=other.at[c],
            send_sem=sketch_send.at[c],
            recv_sem=sketch_recv.at[c],
            device_id=row_peer_sa,
            device_id_type=MESH,
        )

    row_peer_sa = (gx, gz, 1 - sa)
    for g, (c0, nc, width) in enumerate(GROUPS):
        arrived(3, g, field3)

        def fourth(x0, g=g, c0=c0, nc=nc, width=width):
            values = stepped(3, g, field3, held_at, True, x0)
            for i in range(nc):
                for b in range(BLOCKS):
                    sketch[c0 + i, b, pl.ds(x0, width)] = values[i, b]

        passes(g, fourth)

        @pl.when(sa == 0)
        def _(c0=c0, nc=nc):
            for c in range(c0, c0 + nc):
                sketch_copy(c).start()

    row_id = lax.broadcasted_iota(jnp.int32, (8, 128), 0)
    lane_id = lax.broadcasted_iota(jnp.int32, (8, 128), 1)

    def place(i, j, acc):
        total = jnp.sum(acc, axis=(0, 1), keepdims=True)
        return jnp.where((row_id == i) & (lane_id == j), total, 0.0)

    def products(c, accs, pairs, left, right):
        def one(x, accs):
            accs = list(accs)
            for half in range(2):
                part = pl.ds(half * 128, 128)
                a = [left[c, b, x, :, part] for b in range(BLOCKS)]
                d = a if right is left else [right[c, b, x, :, part] for b in range(BLOCKS)]
                for n, (i, j) in enumerate(pairs):
                    accs[n] = accs[n] + a[i] * d[j]
            return tuple(accs)

        return lax.fori_loop(0, CELLS, one, accs)

    own_pairs = [(i, j) for i in range(BLOCKS) for j in range(i, BLOCKS)]
    all_pairs = [(i, j) for i in range(BLOCKS) for j in range(BLOCKS)]
    zero = jnp.zeros((8, 128), jnp.float32)
    accs = tuple(zero for _ in own_pairs)
    for c in (2, 0, 1):
        accs = products(c, accs, own_pairs, sketch, sketch)
    tile = zero
    for n, (i, j) in enumerate(own_pairs):
        tile = tile + place(i + 4 * sa, j + 4 * sa, accs[n])
    for b in range(BLOCKS):
        square = squares[b]
        tile = tile + place(b + 4 * sa, 8, square[:, :128] + square[:, 128:])
    local_gram[...] = tile

    @pl.when(sa == 1)
    def _():
        accs = tuple(zero for _ in all_pairs)
        for c in (2, 0, 1):
            sketch_copy(c).wait_recv()
            accs = products(c, accs, all_pairs, other, sketch)
        tile = zero
        for n, (i, j) in enumerate(all_pairs):
            tile = tile + place(i, j + 4, accs[n])
        local_gram[...] += tile

    def sums(first_sem, buffer, me, peer, count):
        return [
            pltpu.make_async_remote_copy(
                src_ref=buffer.at[me],
                dst_ref=buffer.at[me],
                send_sem=sum_send.at[first_sem + d],
                recv_sem=sum_recv.at[first_sem + d],
                device_id=peer(d + 1),
                device_id_type=MESH,
            )
            for d in range(count - 1)
        ]

    total = local_gram[...]
    levels = [
        (0, row_sums, rank, row_peer, 8),
        (7, y_sums, y, y_peer, 4),
        (10, z_sums, gx, z_peer, 4),
    ]
    for first_sem, buffer, me, peer, count in levels:
        buffer[me] = total
        for copy in sums(first_sem, buffer, me, peer, count):
            copy.start()
        for copy in sums(first_sem, buffer, me, peer, count):
            copy.wait_recv()
        total = buffer[0]
        for k in range(1, count):
            total = total + buffer[k]

    for j in range(9):
        turned = total if j == 0 else pltpu.roll(total, 128 - j, 1)
        splats[j] = jnp.broadcast_to(turned[:, 0:1], (8, 128))
    scale = [jnp.sqrt(splats[8, i : i + 1] / entries + 1e-06) for i in range(8)]
    rows = []
    for p in range(8):
        current = {
            j: splats[j, p : p + 1] / entries / (scale[p] * scale[j]) for j in range(p, 8)
        }
        for q in range(p):
            current = {j: current[j] - rows[q][p] * rows[q][j] for j in current}
        root = jnp.sqrt(current[p])
        rows.append({j: current[j] / root for j in current})
    inverse = [None] * 8
    for p in range(7, -1, -1):
        current = {
            j: jnp.full((1, 128), 1.0 if j == p else 0.0, jnp.float32) for j in range(p, 8)
        }
        for q in range(p + 1, 8):
            for j in range(q, 8):
                current[j] = current[j] - rows[p][q] * inverse[q][j]
        inverse[p] = {j: current[j] / rows[p][p] for j in current}
    tile = zero
    for i in range(8):
        for j in range(i, 8):
            tile = tile + jnp.where((row_id == i) & (lane_id == j), rows[i][j], 0.0)
            coefs[i, pl.ds(j, 1)] = inverse[i][j] / scale[i]
    factor_out[...] = tile[:, :8]

    def stores():
        return [
            pltpu.make_async_copy(held.at[c], basis.at[c], store_sem.at[c]) for c in range(3)
        ]

    def write_basis(first, sources):
        weights = [
            [
                jnp.broadcast_to(coefs[i, pl.ds(first + j, 1)], (8, 128))
                if i <= first + j
                else None
                for j in range(BLOCKS)
            ]
            for i in range(len(sources) * BLOCKS)
        ]

        for c in range(3):

            def one(x, carry):
                for half in range(2):
                    part = pl.ds(half * 128, 128)
                    values = [s[c, b, x, :, part] for s in sources for b in range(BLOCKS)]
                    for j in range(BLOCKS):
                        acc = None
                        for i, value in enumerate(values):
                            if weights[i][j] is not None:
                                term = weights[i][j] * value
                                acc = term if acc is None else acc + term
                        held[c, j, x, :, part] = acc
                return carry

            lax.fori_loop(0, CELLS, one, 0)
            stores()[c].start()

    @pl.when(sa == 0)
    def _():
        write_basis(0, [sketch])

    @pl.when(sa == 1)
    def _():
        write_basis(4, [other, sketch])

    for copy in stores():
        copy.wait()
    for e, field in enumerate((field0, field1, field2, field3)):
        for g in range(2):
            for copy in halo_copies(e, g, field):
                copy.wait_send()

    @pl.when(sa == 0)
    def _():
        for c in range(3):
            sketch_copy(c).wait_send()

    for first_sem, buffer, me, peer, count in levels:
        for copy in sums(first_sem, buffer, me, peer, count):
            copy.wait_send()


def shards(forcing, velocity, wall_solve):
    f32, bf16 = jnp.float32, jnp.bfloat16
    entries = (
        3
        * forcing.shape[2]
        * lax.axis_size("gx")
        * forcing.shape[3]
        * lax.axis_size("gz")
        * forcing.shape[4]
    )
    tile = (3, BLOCKS, CELLS, 8, NY)
    padded = (3, BLOCKS, CELLS + 2, 8, NY)
    edges = (4, 2, 3, BLOCKS, CELLS, 1, NY)
    vmem = pl.BlockSpec(memory_space=pltpu.VMEM)
    hbm = pl.BlockSpec(memory_space=pl.ANY)
    return pl.pallas_call(
        functools.partial(kernel, float(entries)),
        out_shape=(jax.ShapeDtypeStruct(tile, f32), jax.ShapeDtypeStruct((8, 8), f32)),
        in_specs=[hbm, vmem, vmem],
        out_specs=(hbm, vmem),
        scratch_shapes=[
            pltpu.VMEM(padded, f32),
            pltpu.VMEM(padded, f32),
            pltpu.VMEM(padded, f32),
            pltpu.VMEM(padded, f32),
            pltpu.VMEM(tile, f32),
            pltpu.VMEM(tile, f32),
            pltpu.VMEM(tile, f32),
            pltpu.VMEM(edges, f32),
            pltpu.VMEM(edges, f32),
            pltpu.VMEM((ROWS, 3 * NY), bf16),
            pltpu.VMEM((3 * NY, NY), bf16),
            pltpu.VMEM((3 * NY, NY), bf16),
            pltpu.VMEM((1, NY), f32),
            pltpu.VMEM((1, NY), f32),
            pltpu.VMEM((BLOCKS, 8, NY), f32),
            pltpu.VMEM((8, 128), f32),
            pltpu.VMEM((8, 8, 128), f32),
            pltpu.VMEM((4, 8, 128), f32),
            pltpu.VMEM((4, 8, 128), f32),
            pltpu.VMEM((9, 8, 128), f32),
            pltpu.VMEM((8, 8, 128), f32),
            pltpu.SemaphoreType.DMA((2,)),
            pltpu.SemaphoreType.DMA((4, 2, 4)),
            pltpu.SemaphoreType.DMA((4, 2, 4)),
            pltpu.SemaphoreType.DMA((3,)),
            pltpu.SemaphoreType.DMA((3,)),
            pltpu.SemaphoreType.DMA((13,)),
            pltpu.SemaphoreType.DMA((13,)),
            pltpu.SemaphoreType.DMA((3,)),
        ],
        compiler_params=pltpu.CompilerParams(
            collective_id=0, has_side_effects=True, vmem_limit_bytes=56 << 20
        ),
        name="sketch",
    )(forcing, velocity.reshape(1, NY), wall_solve)


def solution(mesh):
    return jax.shard_map(
        shards,
        mesh=mesh,
        in_specs=(P(None, "sa", "gx", "gz", None), P(), P()),
        out_specs=(P(None, "sa", "gx", "gz", None), P()),
        check_vma=False,
    )
```

time: 545 us -> 139 us (0.26)
  blocking collectives: 232 us -> 0 us
  Pallas kernels: 0 us -> 131 us
  waiting for transfers between devices: 128 us -> 0 us
  other arithmetic: 74.8 us -> 0 us
  starting transfers between devices: 31 us -> 0 us
  matrix products: 30.3 us -> 0 us
  between operations: 20 us -> 0.65 us
  local copies, waits for them, and re-layouts: 20.9 us -> 4.35 us
    psum x2 -> x0, blocking collectives: 232 us -> none  [the longest x1 166 us: shards(): totals = lax.psum(partial_value, ('gx', 'gz'))]
    pallas_call x0 -> x1, Pallas kernels: none -> 131 us  [shards(): pl.pallas_call(functools.partial(kernel, float(entries)), out_shape=(jax....]
    all_gather x1 -> x0, waiting for transfers between devices: 81.8 us -> none  [shards(): gathered = lax.all_gather(current, 'sa', axis=1, tiled=True)]
    ppermute x16 -> x0, waiting for transfers between devices: 46 us -> none  [the longest x8 32.8 us: extended(): lax.ppermute(head, axis, [((i + 1) % count, i) for i in range(count)])]
    div x10 -> x0, other arithmetic: 39.7 us -> none  [the longest x1 22.6 us: upper_inverse(): row_list[pivot_index] = current_row / factor[pivot_index, pivot_index]]
    ppermute x16 -> x0, starting transfers between devices: 31 us -> none  [the longest x8 19.8 us: extended(): lax.ppermute(head, axis, [((i + 1) % count, i) for i in range(count)])]
    dot_general x6 -> x0, matrix products: 30.3 us -> none  [the longest x1 11.2 us: shards(): jnp.einsum('cixzy,ij->cjxzy', gathered, own_coef, precision=lax.Precision...]
    sub x8 -> x0, other arithmetic: 18.3 us -> none  [the longest x7 17.7 us: upper_factor(): current_row - row_list[other_index][pivot_index] * row_list[other_index]]
  transfers between devices with their start and end apart: 17 -> 0, of which waited for: 15 -> 0; matrix products, arithmetic and copies ran while one was open for 1% -> 0% of each run, Pallas kernels for 0% -> 0%
where the time goes in v1:
time: 139 us; the launch traced here: 136 us
  Pallas kernels  131 us (94%)
  local copies, waits for them, and re-layouts  4.35 us (3%)
    pallas_call x1, Pallas kernels, shards(): pl.pallas_call(functools.partial(kernel, float(entries)), out_shape=(jax....  131 us
    unnamed x4, local copies, waits for them, and re-layouts  4.35 us

profile of v1, /device:TPU:1, one launch (start us, length us, event | category | flops | bytes accessed | tf_op | source)
XLA Modules:
  0.0 136.2 jit_solution(14397554616238811793)
XLA Ops:
  0.6 131.2 %sketch.1 = (f32[3,4,32,8,256]{4,3,2,1,0:T(8,128)}, f32[8,8]{1,0:T(8,128)}) custom-call(f32[3,4,32,8,256]{4,3,2,1,0:T(8,128)} %forcing.1, f32[1,256]{1,0:T(1,128)} %bitcast.1, f32[256,256]{1,0:T(8,128)} %wall.1), custom_call_target="tpu_custom_call" | custom-call | tf_op jit(solution)/shard_map/sketch/pallas_call | solution.py:499
  131.8 0.0 copy-start
  131.8 3.8 %copy.7 = f32[3,4,32,8,256]{4,3,2,1,0:T(8,128)} copy(f32[3,4,32,8,256]{4,3,2,1,0:T(8,128)} %get-tuple-element.4) | data formatting | bytes 6291456
  135.6 0.0 copy-done
  135.6 0.6 copy.8
Async XLA Ops:
  131.8 3.8 %copy-start = (f32[8,8]{1,0:T(8,128)S(1)}, f32[8,8]{1,0:T(8,128)}, u32[]{:S(2)}) copy-start(f32[8,8]{1,0:T(8,128)} %get-tuple-element.5) | copy-start | bytes 772

commit v2 on v1

--- a/solution.py
+++ b/solution.py
@@ -46,10 +46,15 @@
     splats,
     coefs,
     load_sem,
+    merge_send,
+    merge_recv,
     send_sem,
     recv_sem,
     sketch_send,
     sketch_recv,
+    relay_send,
+    near_send,
+    own_sem,
     sum_send,
     sum_recv,
     store_sem,
@@ -71,24 +76,67 @@
     def gz_peer(offset):
         return (gx, lax.rem(gz + offset + 16, 16), sa)
 
-    def loads():
-        return [
-            pltpu.make_async_copy(
-                forcing.at[pl.ds(c0, nc)],
-                field0.at[pl.ds(c0, nc), :, pl.ds(1, CELLS)],
+    near = in_row + 1 - 2 * lax.rem(in_row, 2)
+    far_first = 2 - 2 * lax.div(in_row, 2)
+    near_first = 2 * lax.div(in_row, 2)
+
+    def load(g, merged):
+        part = pl.ds(*GROUPS[g][:2])
+        if merged:
+            return pltpu.make_async_copy(
+                forcing.at[part, in_row],
+                field0.at[part, in_row, pl.ds(1, CELLS)],
                 load_sem.at[g],
             )
-            for g, (c0, nc, _) in enumerate(GROUPS)
-        ]
-
-    for copy in loads():
-        copy.start()
+        return pltpu.make_async_copy(
+            forcing.at[part], field0.at[part, :, pl.ds(1, CELLS)], load_sem.at[g]
+        )
+
+    def remote(src, dst, sent, received, device):
+        return pltpu.make_async_remote_copy(
+            src_ref=src,
+            dst_ref=dst,
+            send_sem=sent,
+            recv_sem=received,
+            device_id=device,
+            device_id_type=MESH,
+        )
+
+    def merge_copy(g, d):
+        part = pl.ds(*GROUPS[g][:2])
+        column = lax.rem(in_row + d, 4)
+        return remote(
+            forcing.at[part, column],
+            field0.at[part, in_row, pl.ds(1, CELLS)],
+            merge_send.at[g, d - 1],
+            merge_recv.at[g, d - 1],
+            (gx, y * 4 + column, sa),
+        )
+
     barrier = pltpu.get_barrier_semaphore()
     peers = [row_peer(d) for d in range(1, 8)]
     peers += [y_peer(d) for d in range(1, 4)] + [z_peer(d) for d in range(1, 4)]
     peers += [gz_peer(1), gz_peer(-1)]
     for peer in peers:
         pl.semaphore_signal(barrier, inc=1, device_id=peer, device_id_type=MESH)
+
+    @pl.when(sa == 1)
+    def _():
+        for g in range(2):
+            load(g, False).start()
+
+    @pl.when(sa == 0)
+    def _():
+        for g in range(2):
+            load(g, True).start()
+
+    pl.semaphore_wait(barrier, len(peers))
+
+    @pl.when(sa == 0)
+    def _():
+        for g in range(2):
+            for d in (2, 3, 1):
+                merge_copy(g, d).start()
 
     row = velocity[...]
     lane = lax.broadcasted_iota(jnp.int32, (1, NY), 1)
@@ -123,32 +171,47 @@
     def product(weights):
         return jnp.dot(lhs[...], weights[...], preferred_element_type=jnp.float32)
 
-    def halo_copies(e, g, field):
-        c0, nc, _ = GROUPS[g]
-        part = pl.ds(c0, nc)
-
-        def remote(k, src, dst, device):
-            return pltpu.make_async_remote_copy(
-                src_ref=src,
-                dst_ref=dst,
-                send_sem=send_sem.at[e, g, k],
-                recv_sem=recv_sem.at[e, g, k],
-                device_id=device,
-                device_id_type=MESH,
-            )
-
+    def halo_copies(e, g, field, merged):
+        part = pl.ds(*GROUPS[g][:2])
+
+        def copy(k, src, dst, device):
+            return remote(src, dst, send_sem.at[e, g, k], recv_sem.at[e, g, k], device)
+
+        if merged:
+            up, down = (edge_out.at[e, k, part, 0] for k in range(2))
+            north, south = (edge_in.at[e, k, part, 0] for k in range(2))
+            ahead, behind = y_peer(1), y_peer(3)
+        else:
+            up, down = (edge_out.at[e, k, part] for k in range(2))
+            north, south = (edge_in.at[e, k, part] for k in range(2))
+            ahead, behind = gz_peer(1), gz_peer(-1)
         return [
-            remote(0, edge_out.at[e, 0, part], edge_in.at[e, 1, part], gz_peer(1)),
-            remote(1, edge_out.at[e, 1, part], edge_in.at[e, 0, part], gz_peer(-1)),
-            remote(2, field.at[part, :, CELLS], field.at[part, :, 0], z_peer(1)),
-            remote(3, field.at[part, :, 1], field.at[part, :, CELLS + 1], z_peer(3)),
+            copy(0, up, south, ahead),
+            copy(1, down, north, behind),
+            copy(2, field.at[part, :, CELLS], field.at[part, :, 0], z_peer(1)),
+            copy(3, field.at[part, :, 1], field.at[part, :, CELLS + 1], z_peer(3)),
         ]
 
-    def put_edges(e, c, b, cells, value):
-        edge_out[e, 0, c, b, cells] = value[:, 7:8, :]
-        edge_out[e, 1, c, b, cells] = value[:, 0:1, :]
-
-    def stepped(e, g, field, extra, adjoint, x0):
+    def put_edges(e, c, b, cells, value, merged):
+        if not merged:
+            edge_out[e, 0, c, b, cells] = value[:, 7:8, :]
+            edge_out[e, 1, c, b, cells] = value[:, 0:1, :]
+        elif b == BLOCKS - 1:
+            edge_out[e, 0, c, 0, cells] = value[:, 7:8, :]
+        elif b == 0:
+            edge_out[e, 1, c, 0, cells] = value[:, 0:1, :]
+
+    def north_row(e, field, c, b, x0, width, merged):
+        if merged and b < BLOCKS - 1:
+            return field[c, b + 1, pl.ds(x0 + 1, width), 0:1, :]
+        return edge_in[e, 0, c, 0 if merged else b, pl.ds(x0, width)]
+
+    def south_row(e, field, c, b, x0, width, merged):
+        if merged and b > 0:
+            return field[c, b - 1, pl.ds(x0 + 1, width), 7:8, :]
+        return edge_in[e, 1, c, 0 if merged else b, pl.ds(x0, width)]
+
+    def stepped(e, g, field, extra, adjoint, x0, merged):
         c0, nc, width = GROUPS[g]
         drift = drift_row[...].reshape(1, 1, NY)
         shear = shear_row[...].reshape(1, 1, NY)
@@ -163,12 +226,9 @@
                 center = centers[i]
                 east = field[c, b, pl.ds(x0 + 2, width)]
                 west = field[c, b, pl.ds(x0, width)]
-                north = jnp.where(
-                    level == 7, edge_in[e, 0, c, b, pl.ds(x0, width)], pltpu.roll(center, 7, 1)
-                )
-                south = jnp.where(
-                    level == 0, edge_in[e, 1, c, b, pl.ds(x0, width)], pltpu.roll(center, 1, 1)
-                )
+                place = (e, field, c, b, x0, width, merged)
+                north = jnp.where(level == 7, north_row(*place), pltpu.roll(center, 7, 1))
+                south = jnp.where(level == 0, south_row(*place), pltpu.roll(center, 1, 1))
                 value = (step_length * viscosity) * ((east + west) + (north + south))
                 value = value + drift * (west - east)
                 if extra is None:
@@ -217,34 +277,12 @@
 
         passes(g, step)
 
-    def put(e, g, field, values, x0):
+    def put(e, g, field, values, x0, merged):
         c0, nc, width = GROUPS[g]
         for i in range(nc):
             for b in range(BLOCKS):
                 field[c0 + i, b, pl.ds(x0 + 1, width)] = values[i, b]
-                put_edges(e, c0 + i, b, pl.ds(x0, width), values[i, b])
-
-    for g, (c0, nc, width) in enumerate(GROUPS):
-        loads()[g].wait()
-
-        def edges(x0, c0=c0, nc=nc, width=width):
-            for c in range(c0, c0 + nc):
-                for b in range(BLOCKS):
-                    put_edges(0, c, b, pl.ds(x0, width), field0[c, b, pl.ds(x0 + 1, width)])
-
-        passes(g, edges)
-        if g == 0:
-            pl.semaphore_wait(barrier, len(peers))
-        for copy in halo_copies(0, g, field0):
-            copy.start()
-
-    def arrived(e, g, field):
-        for copy in halo_copies(e, g, field):
-            copy.wait_recv()
-
-    def send(e, g, field):
-        for copy in halo_copies(e, g, field):
-            copy.start()
+                put_edges(e, c0 + i, b, pl.ds(x0, width), values[i, b], merged)
 
     def forcing_at(c, b, x0, width):
         return field0[c, b, pl.ds(x0 + 1, width)]
@@ -252,127 +290,192 @@
     def held_at(c, b, x0, width):
         return held[c, b, pl.ds(x0, width)]
 
-    for g in range(2):
-        arrived(0, g, field0)
-
-        def first(x0, spread, solved, g=g):
-            spread(stepped(0, g, field0, None, False, x0))
-            put(1, g, field1, solved(solve), x0)
-
-        run_group(g, first)
-        send(1, g, field1)
-
-    for g in range(2):
-        arrived(1, g, field1)
-
-        def second(x0, spread, solved, g=g):
-            c0, nc, width = GROUPS[g]
-            spread(stepped(1, g, field1, forcing_at, False, x0))
-            values = solved(solve)
-            for b in range(BLOCKS):
-                total = squares[b]
+    def chain(merged, finished):
+        def arrived(e, g, field):
+            for copy in halo_copies(e, g, field, merged):
+                copy.wait_recv()
+
+        def send(e, g, field):
+            for copy in halo_copies(e, g, field, merged):
+                copy.start()
+
+        for g, (c0, nc, width) in enumerate(GROUPS):
+            load(g, merged).wait()
+            if merged:
+                for d in (1, 2, 3):
+                    merge_copy(g, d).wait_recv()
+
+            def edges(x0, c0=c0, nc=nc, width=width):
+                for c in range(c0, c0 + nc):
+                    for b in (0, BLOCKS - 1) if merged else range(BLOCKS):
+                        cells = pl.ds(x0, width)
+                        put_edges(0, c, b, cells, field0[c, b, pl.ds(x0 + 1, width)], merged)
+
+            passes(g, edges)
+            send(0, g, field0)
+
+        for g in range(2):
+            arrived(0, g, field0)
+
+            def first(x0, spread, solved, g=g):
+                spread(stepped(0, g, field0, None, False, x0, merged))
+                put(1, g, field1, solved(solve), x0, merged)
+
+            run_group(g, first)
+            send(1, g, field1)
+
+        for g in range(2):
+            arrived(1, g, field1)
+
+            def second(x0, spread, solved, g=g):
+                c0, nc, width = GROUPS[g]
+                spread(stepped(1, g, field1, forcing_at, False, x0, merged))
+                values = solved(solve)
+                for b in range(BLOCKS):
+                    total = squares[b]
+                    for i in range(nc):
+                        value = values[i, b]
+                        held[c0 + i, b, pl.ds(x0, width)] = value
+                        total = total + jnp.sum(value * value, axis=0)
+                    squares[b] = total
+                spread(values)
+                put(2, g, field2, solved(solve_t), x0, merged)
+
+            run_group(g, second)
+            send(2, g, field2)
+
+        for g in range(2):
+            arrived(2, g, field2)
+
+            def third(x0, spread, solved, g=g):
+                spread(stepped(2, g, field2, held_at, True, x0, merged))
+                put(3, g, field3, solved(solve_t), x0, merged)
+
+            run_group(g, third)
+            send(3, g, field3)
+
+        for g, (c0, nc, width) in enumerate(GROUPS):
+            arrived(3, g, field3)
+
+            def fourth(x0, g=g, c0=c0, nc=nc, width=width):
+                values = stepped(3, g, field3, held_at, True, x0, merged)
                 for i in range(nc):
-                    value = values[i, b]
-                    held[c0 + i, b, pl.ds(x0, width)] = value
-                    total = total + jnp.sum(value * value, axis=0)
-                squares[b] = total
-            spread(values)
-            put(2, g, field2, solved(solve_t), x0)
-
-        run_group(g, second)
-        send(2, g, field2)
-
-    for g in range(2):
-        arrived(2, g, field2)
-
-        def third(x0, spread, solved, g=g):
-            spread(stepped(2, g, field2, held_at, True, x0))
-            put(3, g, field3, solved(solve_t), x0)
-
-        run_group(g, third)
-        send(3, g, field3)
-
-    def sketch_copy(c):
-        return pltpu.make_async_remote_copy(
-            src_ref=sketch.at[c],
-            dst_ref=other.at[c],
-            send_sem=sketch_send.at[c],
-            recv_sem=sketch_recv.at[c],
-            device_id=row_peer_sa,
-            device_id_type=MESH,
+                    for b in range(BLOCKS):
+                        sketch[c0 + i, b, pl.ds(x0, width)] = values[i, b]
+
+            passes(g, fourth)
+            for c in range(c0, c0 + nc):
+                finished(c)
+
+    def spread_copy(c, t):
+        return remote(
+            sketch.at[c, t],
+            other.at[c, in_row],
+            sketch_send.at[c, t],
+            sketch_recv.at[c, in_row],
+            (gx, y * 4 + t, 1),
         )
 
-    row_peer_sa = (gx, gz, 1 - sa)
-    for g, (c0, nc, width) in enumerate(GROUPS):
-        arrived(3, g, field3)
-
-        def fourth(x0, g=g, c0=c0, nc=nc, width=width):
-            values = stepped(3, g, field3, held_at, True, x0)
-            for i in range(nc):
-                for b in range(BLOCKS):
-                    sketch[c0 + i, b, pl.ds(x0, width)] = values[i, b]
-
-        passes(g, fourth)
-
-        @pl.when(sa == 0)
-        def _(c0=c0, nc=nc):
-            for c in range(c0, c0 + nc):
-                sketch_copy(c).start()
+    def near_copy(c):
+        return remote(
+            sketch.at[c, near],
+            other.at[c, in_row],
+            near_send.at[c],
+            sketch_recv.at[c, in_row],
+            (gx, y * 4 + near, 0),
+        )
+
+    def relay_copy(c, k):
+        return remote(
+            other.at[c, k],
+            other.at[c, k],
+            relay_send.at[c, k],
+            sketch_recv.at[c, k],
+            (gx, gz, 0),
+        )
+
+    def own_copy(c):
+        return pltpu.make_async_copy(sketch.at[c, in_row], other.at[c, in_row], own_sem.at[c])
+
+    def sketch_wait(c, k):
+        remote(
+            other.at[c, k],
+            other.at[c, k],
+            relay_send.at[c, k],
+            sketch_recv.at[c, k],
+            (gx, gz, 1 - sa),
+        ).wait_recv()
+
+    def give(c):
+        for k in range(2):
+            spread_copy(c, far_first + k).start()
+        for k in range(2):
+            spread_copy(c, near_first + k).start()
+        near_copy(c).start()
+        own_copy(c).start()
 
     row_id = lax.broadcasted_iota(jnp.int32, (8, 128), 0)
     lane_id = lax.broadcasted_iota(jnp.int32, (8, 128), 1)
+    zero = jnp.zeros((8, 128), jnp.float32)
 
     def place(i, j, acc):
         total = jnp.sum(acc, axis=(0, 1), keepdims=True)
         return jnp.where((row_id == i) & (lane_id == j), total, 0.0)
 
-    def products(c, accs, pairs, left, right):
+    def products(c, accs, pairs, sources):
         def one(x, accs):
             accs = list(accs)
             for half in range(2):
                 part = pl.ds(half * 128, 128)
-                a = [left[c, b, x, :, part] for b in range(BLOCKS)]
-                d = a if right is left else [right[c, b, x, :, part] for b in range(BLOCKS)]
+                values = [s[c, b, x, :, part] for s in sources for b in range(BLOCKS)]
                 for n, (i, j) in enumerate(pairs):
-                    accs[n] = accs[n] + a[i] * d[j]
+                    accs[n] = accs[n] + values[i] * values[j]
             return tuple(accs)
 
         return lax.fori_loop(0, CELLS, one, accs)
 
-    own_pairs = [(i, j) for i in range(BLOCKS) for j in range(i, BLOCKS)]
-    all_pairs = [(i, j) for i in range(BLOCKS) for j in range(BLOCKS)]
-    zero = jnp.zeros((8, 128), jnp.float32)
-    accs = tuple(zero for _ in own_pairs)
-    for c in (2, 0, 1):
-        accs = products(c, accs, own_pairs, sketch, sketch)
-    tile = zero
-    for n, (i, j) in enumerate(own_pairs):
-        tile = tile + place(i + 4 * sa, j + 4 * sa, accs[n])
-    for b in range(BLOCKS):
-        square = squares[b]
-        tile = tile + place(b + 4 * sa, 8, square[:, :128] + square[:, 128:])
-    local_gram[...] = tile
+    @pl.when(sa == 0)
+    def _():
+        chain(True, give)
+        square = squares[0] + squares[1] + squares[2] + squares[3]
+        local_gram[...] = place(in_row, 8, square[:, :128] + square[:, 128:])
 
     @pl.when(sa == 1)
     def _():
-        accs = tuple(zero for _ in all_pairs)
+        chain(False, lambda c: None)
+        own_pairs = [(i, j) for i in range(BLOCKS) for j in range(i, BLOCKS)]
+        accs = tuple(zero for _ in own_pairs)
         for c in (2, 0, 1):
-            sketch_copy(c).wait_recv()
-            accs = products(c, accs, all_pairs, other, sketch)
+            accs = products(c, accs, own_pairs, [sketch])
         tile = zero
-        for n, (i, j) in enumerate(all_pairs):
-            tile = tile + place(i, j + 4, accs[n])
+        for n, (i, j) in enumerate(own_pairs):
+            tile = tile + place(i + 4, j + 4, accs[n])
+        for b in range(BLOCKS):
+            square = squares[b]
+            tile = tile + place(b + 4, 8, square[:, :128] + square[:, 128:])
+        local_gram[...] = tile
+        pairs = [(i, j) for i in range(BLOCKS) for j in range(i, 2 * BLOCKS)]
+        accs = tuple(zero for _ in pairs)
+        for c in (2, 0, 1):
+            for k in range(2):
+                sketch_wait(c, far_first + k)
+                relay_copy(c, far_first + k).start()
+            for k in range(2):
+                sketch_wait(c, near_first + k)
+            accs = products(c, accs, pairs, [other, sketch])
+        tile = zero
+        for n, (i, j) in enumerate(pairs):
+            tile = tile + place(i, j, accs[n])
         local_gram[...] += tile
 
     def sums(first_sem, buffer, me, peer, count):
         return [
-            pltpu.make_async_remote_copy(
-                src_ref=buffer.at[me],
-                dst_ref=buffer.at[me],
-                send_sem=sum_send.at[first_sem + d],
-                recv_sem=sum_recv.at[first_sem + d],
-                device_id=peer(d + 1),
-                device_id_type=MESH,
+            remote(
+                buffer.at[me],
+                buffer.at[me],
+                sum_send.at[first_sem + d],
+                sum_recv.at[first_sem + d],
+                peer(d + 1),
             )
             for d in range(count - 1)
         ]
@@ -422,12 +525,10 @@
             coefs[i, pl.ds(j, 1)] = inverse[i][j] / scale[i]
     factor_out[...] = tile[:, :8]
 
-    def stores():
-        return [
-            pltpu.make_async_copy(held.at[c], basis.at[c], store_sem.at[c]) for c in range(3)
-        ]
-
-    def write_basis(first, sources):
+    def store(c):
+        return pltpu.make_async_copy(held.at[c], basis.at[c], store_sem.at[c])
+
+    def write_basis(first, sources, ready):
         weights = [
             [
                 jnp.broadcast_to(coefs[i, pl.ds(first + j, 1)], (8, 128))
@@ -438,7 +539,8 @@
             for i in range(len(sources) * BLOCKS)
         ]
 
-        for c in range(3):
+        for c in (2, 0, 1):
+            ready(c)
 
             def one(x, carry):
                 for half in range(2):
@@ -454,28 +556,41 @@
                 return carry
 
             lax.fori_loop(0, CELLS, one, 0)
-            stores()[c].start()
+            store(c).start()
+
+    def drain(merged):
+        for e, field in enumerate((field0, field1, field2, field3)):
+            for g in range(2):
+                for copy in halo_copies(e, g, field, merged):
+                    copy.wait_send()
 
     @pl.when(sa == 0)
     def _():
-        write_basis(0, [sketch])
+        def ready(c):
+            own_copy(c).wait()
+            for d in (1, 2, 3):
+                sketch_wait(c, lax.rem(in_row + d, 4))
+
+        write_basis(0, [other], ready)
+        drain(True)
+        for g in range(2):
+            for d in (1, 2, 3):
+                merge_copy(g, d).wait_send()
+        for c in range(3):
+            for t in range(BLOCKS):
+                spread_copy(c, t).wait_send()
+            near_copy(c).wait_send()
 
     @pl.when(sa == 1)
     def _():
-        write_basis(4, [other, sketch])
-
-    for copy in stores():
-        copy.wait()
-    for e, field in enumerate((field0, field1, field2, field3)):
-        for g in range(2):
-            for copy in halo_copies(e, g, field):
-                copy.wait_send()
-
-    @pl.when(sa == 0)
-    def _():
+        write_basis(4, [other, sketch], lambda c: None)
+        drain(False)
         for c in range(3):
-            sketch_copy(c).wait_send()
-
+            for k in range(2):
+                relay_copy(c, far_first + k).wait_send()
+
+    for c in range(3):
+        store(c).wait()
     for first_sem, buffer, me, peer, count in levels:
         for copy in sums(first_sem, buffer, me, peer, count):
             copy.wait_send()
@@ -524,8 +639,13 @@
             pltpu.VMEM((9, 8, 128), f32),
             pltpu.VMEM((8, 8, 128), f32),
             pltpu.SemaphoreType.DMA((2,)),
+            pltpu.SemaphoreType.DMA((2, 3)),
+            pltpu.SemaphoreType.DMA((2, 3)),
             pltpu.SemaphoreType.DMA((4, 2, 4)),
             pltpu.SemaphoreType.DMA((4, 2, 4)),
+            pltpu.SemaphoreType.DMA((3, 4)),
+            pltpu.SemaphoreType.DMA((3, 4)),
+            pltpu.SemaphoreType.DMA((3, 4)),
             pltpu.SemaphoreType.DMA((3,)),
             pltpu.SemaphoreType.DMA((3,)),
             pltpu.SemaphoreType.DMA((13,)),

time: 139 us -> 128 us (0.921)
  Pallas kernels: 131 us -> 120 us
    pallas_call x1, Pallas kernels: 131 us -> 120 us  [shards(): pl.pallas_call(functools.partial(kernel, float(entries)), out_shape=(jax....]
where the time goes in v2:
time: 128 us; the launch traced here: 125 us
  Pallas kernels  120 us (94%)
  local copies, waits for them, and re-layouts  4.35 us (3%)
    pallas_call x1, Pallas kernels, shards(): pl.pallas_call(functools.partial(kernel, float(entries)), out_shape=(jax....  120 us
    unnamed x4, local copies, waits for them, and re-layouts  4.35 us

profile of v2, /device:TPU:1, one launch (start us, length us, event | category | flops | bytes accessed | tf_op | source)
XLA Modules:
  0.0 125.3 jit_solution(10113266759505058349)
XLA Ops:
  0.6 120.3 %sketch.1 = (f32[3,4,32,8,256]{4,3,2,1,0:T(8,128)}, f32[8,8]{1,0:T(8,128)}) custom-call(f32[3,4,32,8,256]{4,3,2,1,0:T(8,128)} %forcing.1, f32[1,256]{1,0:T(1,128)} %bitcast.1, f32[256,256]{1,0:T(8,128)} %wall.1), custom_call_target="tpu_custom_call" | custom-call | tf_op jit(solution)/shard_map/sketch/pallas_call | solution.py:614
  120.9 0.0 copy-start
  120.9 3.8 %copy.7 = f32[3,4,32,8,256]{4,3,2,1,0:T(8,128)} copy(f32[3,4,32,8,256]{4,3,2,1,0:T(8,128)} %get-tuple-element.4) | data formatting | bytes 6291456
  124.7 0.0 copy-done
  124.7 0.6 copy.8
Async XLA Ops:
  120.9 3.8 %copy-start = (f32[8,8]{1,0:T(8,128)S(1)}, f32[8,8]{1,0:T(8,128)}, u32[]{:S(2)}) copy-start(f32[8,8]{1,0:T(8,128)} %get-tuple-element.5) | copy-start | bytes 772

commit v3 on v2

--- a/solution.py
+++ b/solution.py
@@ -171,26 +171,24 @@
     def product(weights):
         return jnp.dot(lhs[...], weights[...], preferred_element_type=jnp.float32)
 
-    def halo_copies(e, g, field, merged):
+    def halo_copy(e, g, field, merged, k):
         part = pl.ds(*GROUPS[g][:2])
-
-        def copy(k, src, dst, device):
-            return remote(src, dst, send_sem.at[e, g, k], recv_sem.at[e, g, k], device)
-
-        if merged:
-            up, down = (edge_out.at[e, k, part, 0] for k in range(2))
-            north, south = (edge_in.at[e, k, part, 0] for k in range(2))
-            ahead, behind = y_peer(1), y_peer(3)
+        if k < 4:
+            half, way = divmod(k, 2)
+            cells = pl.ds(half * (CELLS // 2), CELLS // 2)
+            if merged:
+                src = edge_out.at[e, way, part, 0, cells]
+                dst = edge_in.at[e, 1 - way, part, 0, cells]
+                device = y_peer(3) if way else y_peer(1)
+            else:
+                src = edge_out.at[e, way, part, :, cells]
+                dst = edge_in.at[e, 1 - way, part, :, cells]
+                device = gz_peer(-1) if way else gz_peer(1)
+        elif k == 4:
+            src, dst, device = field.at[part, :, CELLS], field.at[part, :, 0], z_peer(1)
         else:
-            up, down = (edge_out.at[e, k, part] for k in range(2))
-            north, south = (edge_in.at[e, k, part] for k in range(2))
-            ahead, behind = gz_peer(1), gz_peer(-1)
-        return [
-            copy(0, up, south, ahead),
-            copy(1, down, north, behind),
-            copy(2, field.at[part, :, CELLS], field.at[part, :, 0], z_peer(1)),
-            copy(3, field.at[part, :, 1], field.at[part, :, CELLS + 1], z_peer(3)),
-        ]
+            src, dst, device = field.at[part, :, 1], field.at[part, :, CELLS + 1], z_peer(3)
+        return remote(src, dst, send_sem.at[e, g, k], recv_sem.at[e, g, k], device)
 
     def put_edges(e, c, b, cells, value, merged):
         if not merged:
@@ -201,17 +199,17 @@
         elif b == 0:
             edge_out[e, 1, c, 0, cells] = value[:, 0:1, :]
 
-    def north_row(e, field, c, b, x0, width, merged):
+    def north_row(e, field, c, b, x0, p0, width, merged):
         if merged and b < BLOCKS - 1:
             return field[c, b + 1, pl.ds(x0 + 1, width), 0:1, :]
-        return edge_in[e, 0, c, 0 if merged else b, pl.ds(x0, width)]
-
-    def south_row(e, field, c, b, x0, width, merged):
+        return edge_in[e, 0, c, 0 if merged else b, pl.ds(p0, width)]
+
+    def south_row(e, field, c, b, x0, p0, width, merged):
         if merged and b > 0:
             return field[c, b - 1, pl.ds(x0 + 1, width), 7:8, :]
-        return edge_in[e, 1, c, 0 if merged else b, pl.ds(x0, width)]
-
-    def stepped(e, g, field, extra, adjoint, x0, merged):
+        return edge_in[e, 1, c, 0 if merged else b, pl.ds(p0, width)]
+
+    def stepped(e, g, field, extra, adjoint, x0, p0, merged):
         c0, nc, width = GROUPS[g]
         drift = drift_row[...].reshape(1, 1, NY)
         shear = shear_row[...].reshape(1, 1, NY)
@@ -226,7 +224,7 @@
                 center = centers[i]
                 east = field[c, b, pl.ds(x0 + 2, width)]
                 west = field[c, b, pl.ds(x0, width)]
-                place = (e, field, c, b, x0, width, merged)
+                place = (e, field, c, b, x0, p0, width, merged)
                 north = jnp.where(level == 7, north_row(*place), pltpu.roll(center, 7, 1))
                 south = jnp.where(level == 0, south_row(*place), pltpu.roll(center, 1, 1))
                 value = (step_length * viscosity) * ((east + west) + (north + south))
@@ -241,48 +239,69 @@
                 out[i, b] = value
         return out
 
-    def passes(g, body):
+    def passes(g, body, merged, source=None, target=None):
         width = GROUPS[g][2]
+        count = CELLS // width
+        if count == 2:
+            needed = {0: (0, 1, 4), 1: (2, 3, 5)}
+            made = {0: (0, 1, 5), 1: (2, 3, 4)}
+        else:
+            needed = {0: (0, 1, 4, 5), 2: (2, 3)}
+            made = {1: (0, 1, 4, 5), 3: (2, 3)}
 
         def one(i, carry):
-            body(pl.multiple_of(i * width, width))
+            if count == 2:
+                x0 = i * width
+            else:
+                x0 = lax.select(i < 2, i * (CELLS - width), (i - 1) * width)
+            if source is not None:
+                for at, copies in needed.items():
+
+                    @pl.when(i == at)
+                    def _(copies=copies):
+                        for k in copies:
+                            halo_copy(*source, merged, k).wait_recv()
+
+            body(pl.multiple_of(x0, width), pl.multiple_of(i * width, width))
+            if target is not None:
+                for at, copies in made.items():
+
+                    @pl.when(i == at)
+                    def _(copies=copies):
+                        for k in copies:
+                            halo_copy(*target, merged, k).start()
+
             return carry
 
-        lax.fori_loop(0, CELLS // width, one, 0)
-
-    def run_group(g, body):
+        lax.fori_loop(0, count, one, 0)
+
+    def run_group(g, body, merged, source, target):
         c0, nc, width = GROUPS[g]
         tile = width * 8
 
-        def step(x0):
-            body(
-                x0,
-                lambda values: [
+        def spread(values):
+            for i in range(nc):
+                for b in range(BLOCKS):
                     split_rows((i * BLOCKS + b) * tile, values[i, b])
-                    for i in range(nc)
-                    for b in range(BLOCKS)
-                ],
-                lambda weights: {
-                    (i, b): value
-                    for prod in [product(weights)]
-                    for i in range(nc)
-                    for b in range(BLOCKS)
-                    for value in [
-                        prod[(i * BLOCKS + b) * tile : (i * BLOCKS + b + 1) * tile].reshape(
-                            width, 8, NY
-                        )
-                    ]
-                },
-            )
-
-        passes(g, step)
-
-    def put(e, g, field, values, x0, merged):
+
+        def solved(weights):
+            prod = product(weights)
+            return {
+                (i, b): prod[(i * BLOCKS + b) * tile : (i * BLOCKS + b + 1) * tile].reshape(
+                    width, 8, NY
+                )
+                for i in range(nc)
+                for b in range(BLOCKS)
+            }
+
+        passes(g, lambda x0, p0: body(x0, p0, spread, solved), merged, source, target)
+
+    def put(e, g, field, values, x0, p0, merged):
         c0, nc, width = GROUPS[g]
         for i in range(nc):
             for b in range(BLOCKS):
                 field[c0 + i, b, pl.ds(x0 + 1, width)] = values[i, b]
-                put_edges(e, c0 + i, b, pl.ds(x0, width), values[i, b], merged)
+                put_edges(e, c0 + i, b, pl.ds(p0, width), values[i, b], merged)
 
     def forcing_at(c, b, x0, width):
         return field0[c, b, pl.ds(x0 + 1, width)]
@@ -291,45 +310,33 @@
         return held[c, b, pl.ds(x0, width)]
 
     def chain(merged, finished):
-        def arrived(e, g, field):
-            for copy in halo_copies(e, g, field, merged):
-                copy.wait_recv()
-
-        def send(e, g, field):
-            for copy in halo_copies(e, g, field, merged):
-                copy.start()
-
-        for g, (c0, nc, width) in enumerate(GROUPS):
+        def start(g):
+            c0, nc, width = GROUPS[g]
             load(g, merged).wait()
             if merged:
                 for d in (1, 2, 3):
                     merge_copy(g, d).wait_recv()
 
-            def edges(x0, c0=c0, nc=nc, width=width):
+            def edges(x0, p0):
                 for c in range(c0, c0 + nc):
                     for b in (0, BLOCKS - 1) if merged else range(BLOCKS):
-                        cells = pl.ds(x0, width)
-                        put_edges(0, c, b, cells, field0[c, b, pl.ds(x0 + 1, width)], merged)
-
-            passes(g, edges)
-            send(0, g, field0)
-
-        for g in range(2):
-            arrived(0, g, field0)
-
-            def first(x0, spread, solved, g=g):
-                spread(stepped(0, g, field0, None, False, x0, merged))
-                put(1, g, field1, solved(solve), x0, merged)
-
-            run_group(g, first)
-            send(1, g, field1)
-
-        for g in range(2):
-            arrived(1, g, field1)
-
-            def second(x0, spread, solved, g=g):
-                c0, nc, width = GROUPS[g]
-                spread(stepped(1, g, field1, forcing_at, False, x0, merged))
+                        value = field0[c, b, pl.ds(x0 + 1, width)]
+                        put_edges(0, c, b, pl.ds(p0, width), value, merged)
+
+            passes(g, edges, merged, target=(0, g, field0))
+
+        def first(g):
+            def body(x0, p0, spread, solved):
+                spread(stepped(0, g, field0, None, False, x0, p0, merged))
+                put(1, g, field1, solved(solve), x0, p0, merged)
+
+            run_group(g, body, merged, (0, g, field0), (1, g, field1))
+
+        def second(g):
+            c0, nc, width = GROUPS[g]
+
+            def body(x0, p0, spread, solved):
+                spread(stepped(1, g, field1, forcing_at, False, x0, p0, merged))
                 values = solved(solve)
                 for b in range(BLOCKS):
                     total = squares[b]
@@ -339,33 +346,37 @@
                         total = total + jnp.sum(value * value, axis=0)
                     squares[b] = total
                 spread(values)
-                put(2, g, field2, solved(solve_t), x0, merged)
-
-            run_group(g, second)
-            send(2, g, field2)
-
-        for g in range(2):
-            arrived(2, g, field2)
-
-            def third(x0, spread, solved, g=g):
-                spread(stepped(2, g, field2, held_at, True, x0, merged))
-                put(3, g, field3, solved(solve_t), x0, merged)
-
-            run_group(g, third)
-            send(3, g, field3)
-
-        for g, (c0, nc, width) in enumerate(GROUPS):
-            arrived(3, g, field3)
-
-            def fourth(x0, g=g, c0=c0, nc=nc, width=width):
-                values = stepped(3, g, field3, held_at, True, x0, merged)
+                put(2, g, field2, solved(solve_t), x0, p0, merged)
+
+            run_group(g, body, merged, (1, g, field1), (2, g, field2))
+
+        def third(g):
+            def body(x0, p0, spread, solved):
+                spread(stepped(2, g, field2, held_at, True, x0, p0, merged))
+                put(3, g, field3, solved(solve_t), x0, p0, merged)
+
+            run_group(g, body, merged, (2, g, field2), (3, g, field3))
+
+        def fourth(g):
+            c0, nc, width = GROUPS[g]
+
+            def body(x0, p0):
+                values = stepped(3, g, field3, held_at, True, x0, p0, merged)
                 for i in range(nc):
                     for b in range(BLOCKS):
                         sketch[c0 + i, b, pl.ds(x0, width)] = values[i, b]
 
-            passes(g, fourth)
+            passes(g, body, merged, source=(3, g, field3))
             for c in range(c0, c0 + nc):
                 finished(c)
+
+        stages = (start, first, second, third, fourth)
+        if merged:
+            order = [(stage, g) for g in range(2) for stage in stages]
+        else:
+            order = [(stage, g) for stage in stages for g in range(2)]
+        for stage, g in order:
+            stage(g)
 
     def spread_copy(c, t):
         return remote(
@@ -561,8 +572,8 @@
     def drain(merged):
         for e, field in enumerate((field0, field1, field2, field3)):
             for g in range(2):
-                for copy in halo_copies(e, g, field, merged):
-                    copy.wait_send()
+                for k in range(6):
+                    halo_copy(e, g, field, merged, k).wait_send()
 
     @pl.when(sa == 0)
     def _():
@@ -641,8 +652,8 @@
             pltpu.SemaphoreType.DMA((2,)),
             pltpu.SemaphoreType.DMA((2, 3)),
             pltpu.SemaphoreType.DMA((2, 3)),
-            pltpu.SemaphoreType.DMA((4, 2, 4)),
-            pltpu.SemaphoreType.DMA((4, 2, 4)),
+            pltpu.SemaphoreType.DMA((4, 2, 6)),
+            pltpu.SemaphoreType.DMA((4, 2, 6)),
             pltpu.SemaphoreType.DMA((3, 4)),
             pltpu.SemaphoreType.DMA((3, 4)),
             pltpu.SemaphoreType.DMA((3, 4)),

time: 128 us -> 117 us (0.914); the launches traced: 125 us -> 116 us
  Pallas kernels: 120 us -> 111 us
    pallas_call x1, Pallas kernels: 120 us -> 111 us  [shards(): pl.pallas_call(functools.partial(kernel, float(entries)), out_shape=(jax....]
where the time goes in v3:
time: 117 us; the launch traced here: 116 us
  Pallas kernels  111 us (95%)
  local copies, waits for them, and re-layouts  4.35 us (4%)
    pallas_call x1, Pallas kernels, shards(): pl.pallas_call(functools.partial(kernel, float(entries)), out_shape=(jax....  111 us
    unnamed x4, local copies, waits for them, and re-layouts  4.35 us

profile of v3, /device:TPU:1, one launch (start us, length us, event | category | flops | bytes accessed | tf_op | source)
XLA Modules:
  0.0 115.6 jit_solution(11966737126636683993)
XLA Ops:
  0.6 110.6 %sketch.1 = (f32[3,4,32,8,256]{4,3,2,1,0:T(8,128)}, f32[8,8]{1,0:T(8,128)}) custom-call(f32[3,4,32,8,256]{4,3,2,1,0:T(8,128)} %forcing.1, f32[1,256]{1,0:T(1,128)} %bitcast.1, f32[256,256]{1,0:T(8,128)} %wall.1), custom_call_target="tpu_custom_call" | custom-call | tf_op jit(solution)/shard_map/sketch/pallas_call | solution.py:625
  111.2 0.0 copy-start
  111.2 3.8 %copy.7 = f32[3,4,32,8,256]{4,3,2,1,0:T(8,128)} copy(f32[3,4,32,8,256]{4,3,2,1,0:T(8,128)} %get-tuple-element.4) | data formatting | bytes 6291456
  115.0 0.0 copy-done
  115.0 0.6 copy.8
Async XLA Ops:
  111.2 3.8 %copy-start = (f32[8,8]{1,0:T(8,128)S(1)}, f32[8,8]{1,0:T(8,128)}, u32[]{:S(2)}) copy-start(f32[8,8]{1,0:T(8,128)} %get-tuple-element.5) | copy-start | bytes 772

commit v4 on v3

--- a/solution.py
+++ b/solution.py
@@ -14,16 +14,16 @@
 BLOCKS = 4
 CELLS = 32
 NY = 256
-ROWS = 512
+HALF = 256
 
 
 def kernel(
-    entries,
     forcing,
     velocity,
     wall,
-    basis,
-    factor_out,
+    other_out,
+    sketch_out,
+    gram_out,
     field0,
     field1,
     field2,
@@ -33,7 +33,8 @@
     other,
     edge_out,
     edge_in,
-    lhs,
+    lhs0,
+    lhs1,
     solve,
     solve_t,
     drift_row,
@@ -41,10 +42,7 @@
     squares,
     local_gram,
     row_sums,
-    y_sums,
-    z_sums,
-    splats,
-    coefs,
+    plane_sums,
     load_sem,
     merge_send,
     merge_recv,
@@ -73,6 +71,10 @@
     def z_peer(offset):
         return (lax.rem(gx + offset, 4), gz, sa)
 
+    def plane_peer(offset):
+        place = lax.rem(gx * 4 + y + offset, 16)
+        return (lax.div(place, 4), lax.rem(place, 4) * 4 + in_row, sa)
+
     def gz_peer(offset):
         return (gx, lax.rem(gz + offset + 16, 16), sa)
 
@@ -115,7 +117,7 @@
 
     barrier = pltpu.get_barrier_semaphore()
     peers = [row_peer(d) for d in range(1, 8)]
-    peers += [y_peer(d) for d in range(1, 4)] + [z_peer(d) for d in range(1, 4)]
+    peers += [plane_peer(d) for d in range(1, 16)]
     peers += [gz_peer(1), gz_peer(-1)]
     for peer in peers:
         pl.semaphore_signal(barrier, inc=1, device_id=peer, device_id_type=MESH)
@@ -134,9 +136,8 @@
 
     @pl.when(sa == 0)
     def _():
-        for g in range(2):
-            for d in (2, 3, 1):
-                merge_copy(g, d).start()
+        for d in (1, 2, 3):
+            merge_copy(1, d).start()
 
     row = velocity[...]
     lane = lax.broadcasted_iota(jnp.int32, (1, NY), 1)
@@ -164,12 +165,17 @@
         flat = value.reshape(rows, NY)
         high = flat.astype(jnp.bfloat16)
         low = (flat - high.astype(jnp.float32)).astype(jnp.bfloat16)
-        lhs[pl.ds(start, rows), pl.ds(0, NY)] = high
-        lhs[pl.ds(start, rows), pl.ds(NY, NY)] = low
-        lhs[pl.ds(start, rows), pl.ds(2 * NY, NY)] = high
+        target = (lhs0, lhs1)[start // HALF]
+        place = pl.ds(start % HALF, rows)
+        target[place, pl.ds(0, NY)] = high
+        target[place, pl.ds(NY, NY)] = low
+        target[place, pl.ds(2 * NY, NY)] = high
 
     def product(weights):
-        return jnp.dot(lhs[...], weights[...], preferred_element_type=jnp.float32)
+        return [
+            jnp.dot(part[...], weights[...], preferred_element_type=jnp.float32)
+            for part in (lhs0, lhs1)
+        ]
 
     def halo_copy(e, g, field, merged, k):
         part = pl.ds(*GROUPS[g][:2])
@@ -286,13 +292,12 @@
 
         def solved(weights):
             prod = product(weights)
-            return {
-                (i, b): prod[(i * BLOCKS + b) * tile : (i * BLOCKS + b + 1) * tile].reshape(
-                    width, 8, NY
-                )
-                for i in range(nc)
-                for b in range(BLOCKS)
-            }
+            out = {}
+            for i in range(nc):
+                for b in range(BLOCKS):
+                    half, first = divmod((i * BLOCKS + b) * tile, HALF)
+                    out[i, b] = prod[half][first : first + tile].reshape(width, 8, NY)
+            return out
 
         passes(g, lambda x0, p0: body(x0, p0, spread, solved), merged, source, target)
 
@@ -309,11 +314,15 @@
     def held_at(c, b, x0, width):
         return held[c, b, pl.ds(x0, width)]
 
-    def chain(merged, finished):
+    def chain(merged):
         def start(g):
             c0, nc, width = GROUPS[g]
             load(g, merged).wait()
             if merged:
+                if g == 1:
+                    for d in (1, 2, 3):
+                        merge_copy(1, d).wait_send()
+                        merge_copy(0, d).start()
                 for d in (1, 2, 3):
                     merge_copy(g, d).wait_recv()
 
@@ -367,16 +376,22 @@
                         sketch[c0 + i, b, pl.ds(x0, width)] = values[i, b]
 
             passes(g, body, merged, source=(3, g, field3))
-            for c in range(c0, c0 + nc):
-                finished(c)
 
         stages = (start, first, second, third, fourth)
         if merged:
-            order = [(stage, g) for g in range(2) for stage in stages]
+            for stage in stages:
+                stage(1)
+            give(0)
+            give(1)
+            for stage in stages[:3]:
+                stage(0)
+            for stage in stages[3:]:
+                stage(0)
+            give(2)
         else:
-            order = [(stage, g) for stage in stages for g in range(2)]
-        for stage, g in order:
-            stage(g)
+            for stage in stages:
+                for g in range(2):
+                    stage(g)
 
     def spread_copy(c, t):
         return remote(
@@ -417,13 +432,25 @@
             (gx, gz, 1 - sa),
         ).wait_recv()
 
-    def give(c):
+    def store(c):
+        return pltpu.make_async_copy(other.at[c], other_out.at[c], store_sem.at[c])
+
+    def store_own(c):
+        return pltpu.make_async_copy(sketch.at[c], sketch_out.at[c], store_sem.at[3 + c])
+
+    def give(c, in_turn=False):
         for k in range(2):
             spread_copy(c, far_first + k).start()
-        for k in range(2):
             spread_copy(c, near_first + k).start()
+            if in_turn and k == 0:
+                spread_copy(c, far_first).wait_send()
+                spread_copy(c, near_first).wait_send()
         near_copy(c).start()
         own_copy(c).start()
+
+    def given(c):
+        for t in range(BLOCKS):
+            spread_copy(c, t).wait_send()
 
     row_id = lax.broadcasted_iota(jnp.int32, (8, 128), 0)
     lane_id = lax.broadcasted_iota(jnp.int32, (8, 128), 1)
@@ -447,16 +474,18 @@
 
     @pl.when(sa == 0)
     def _():
-        chain(True, give)
+        chain(True)
         square = squares[0] + squares[1] + squares[2] + squares[3]
         local_gram[...] = place(in_row, 8, square[:, :128] + square[:, 128:])
 
     @pl.when(sa == 1)
     def _():
-        chain(False, lambda c: None)
+        chain(False)
+        for c in range(3):
+            store_own(c).start()
         own_pairs = [(i, j) for i in range(BLOCKS) for j in range(i, BLOCKS)]
         accs = tuple(zero for _ in own_pairs)
-        for c in (2, 0, 1):
+        for c in range(3):
             accs = products(c, accs, own_pairs, [sketch])
         tile = zero
         for n, (i, j) in enumerate(own_pairs):
@@ -467,12 +496,13 @@
         local_gram[...] = tile
         pairs = [(i, j) for i in range(BLOCKS) for j in range(i, 2 * BLOCKS)]
         accs = tuple(zero for _ in pairs)
-        for c in (2, 0, 1):
+        for c in range(3):
             for k in range(2):
                 sketch_wait(c, far_first + k)
                 relay_copy(c, far_first + k).start()
             for k in range(2):
                 sketch_wait(c, near_first + k)
+            store(c).start()
             accs = products(c, accs, pairs, [other, sketch])
         tile = zero
         for n, (i, j) in enumerate(pairs):
@@ -491,11 +521,17 @@
             for d in range(count - 1)
         ]
 
+    def collect():
+        for c in range(3):
+            own_copy(c).wait()
+            for d in (1, 2, 3):
+                sketch_wait(c, lax.rem(in_row + d, 4))
+            store(c).start()
+
     total = local_gram[...]
     levels = [
         (0, row_sums, rank, row_peer, 8),
-        (7, y_sums, y, y_peer, 4),
-        (10, z_sums, gx, z_peer, 4),
+        (7, plane_sums, gx * 4 + y, plane_peer, 16),
     ]
     for first_sem, buffer, me, peer, count in levels:
         buffer[me] = total
@@ -507,6 +543,66 @@
         for k in range(1, count):
             total = total + buffer[k]
 
+    pl.when(sa == 0)(collect)
+
+    gram_out[...] = total
+
+    def drain(merged):
+        for e, field in enumerate((field0, field1, field2, field3)):
+            for g in range(2):
+                for k in range(6):
+                    halo_copy(e, g, field, merged, k).wait_send()
+
+    @pl.when(sa == 0)
+    def _():
+        drain(True)
+        for d in (1, 2, 3):
+            merge_copy(0, d).wait_send()
+        given(0)
+        given(1)
+        given(2)
+        for c in range(3):
+            near_copy(c).wait_send()
+
+    @pl.when(sa == 1)
+    def _():
+        for c in range(3):
+            store_own(c).wait()
+        drain(False)
+        for c in range(3):
+            for k in range(2):
+                relay_copy(c, far_first + k).wait_send()
+
+    for c in range(3):
+        store(c).wait()
+    for first_sem, buffer, me, peer, count in levels:
+        for copy in sums(first_sem, buffer, me, peer, count):
+            copy.wait_send()
+
+
+def basis_kernel(
+    entries, low, high, gram, basis, factor_out, splats, coefs, first, second, result, sems
+):
+    sa = lax.axis_index("sa")
+
+    def load(c, k):
+        src, dst = ((low, first), (high, second))[k]
+        return pltpu.make_async_copy(src.at[c], dst.at[c], sems.at[3 * k + c])
+
+    def store(c):
+        return pltpu.make_async_copy(result.at[c], basis.at[c], sems.at[6 + c])
+
+    for c in range(3):
+        load(c, 0).start()
+
+    @pl.when(sa == 1)
+    def _():
+        for c in range(3):
+            load(c, 1).start()
+
+    total = gram[...]
+    row_id = lax.broadcasted_iota(jnp.int32, (8, 128), 0)
+    lane_id = lax.broadcasted_iota(jnp.int32, (8, 128), 1)
     for j in range(9):
         turned = total if j == 0 else pltpu.roll(total, 128 - j, 1)
         splats[j] = jnp.broadcast_to(turned[:, 0:1], (8, 128))
@@ -529,82 +625,47 @@
             for j in range(q, 8):
                 current[j] = current[j] - rows[p][q] * inverse[q][j]
         inverse[p] = {j: current[j] / rows[p][p] for j in current}
-    tile = zero
+    tile = jnp.zeros((8, 128), jnp.float32)
     for i in range(8):
         for j in range(i, 8):
             tile = tile + jnp.where((row_id == i) & (lane_id == j), rows[i][j], 0.0)
             coefs[i, pl.ds(j, 1)] = inverse[i][j] / scale[i]
     factor_out[...] = tile[:, :8]
 
-    def store(c):
-        return pltpu.make_async_copy(held.at[c], basis.at[c], store_sem.at[c])
-
-    def write_basis(first, sources, ready):
-        weights = [
-            [
-                jnp.broadcast_to(coefs[i, pl.ds(first + j, 1)], (8, 128))
-                if i <= first + j
-                else None
-                for j in range(BLOCKS)
-            ]
-            for i in range(len(sources) * BLOCKS)
-        ]
-
-        for c in (2, 0, 1):
-            ready(c)
+    def combine(start, sources):
+        weights = {
+            (i, j): jnp.broadcast_to(coefs[i, pl.ds(start + j, 1)], (8, 128))
+            for j in range(BLOCKS)
+            for i in range(start + j + 1)
+        }
+        for c in range(3):
+            for k in range(len(sources)):
+                load(c, k).wait()
 
             def one(x, carry):
                 for half in range(2):
                     part = pl.ds(half * 128, 128)
                     values = [s[c, b, x, :, part] for s in sources for b in range(BLOCKS)]
                     for j in range(BLOCKS):
-                        acc = None
-                        for i, value in enumerate(values):
-                            if weights[i][j] is not None:
-                                term = weights[i][j] * value
-                                acc = term if acc is None else acc + term
-                        held[c, j, x, :, part] = acc
+                        acc = weights[0, j] * values[0]
+                        for i in range(1, start + j + 1):
+                            acc = acc + weights[i, j] * values[i]
+                        result[c, j, x, :, part] = acc
                 return carry
 
             lax.fori_loop(0, CELLS, one, 0)
             store(c).start()
 
-    def drain(merged):
-        for e, field in enumerate((field0, field1, field2, field3)):
-            for g in range(2):
-                for k in range(6):
-                    halo_copy(e, g, field, merged, k).wait_send()
-
     @pl.when(sa == 0)
     def _():
-        def ready(c):
-            own_copy(c).wait()
-            for d in (1, 2, 3):
-                sketch_wait(c, lax.rem(in_row + d, 4))
-
-        write_basis(0, [other], ready)
-        drain(True)
-        for g in range(2):
-            for d in (1, 2, 3):
-                merge_copy(g, d).wait_send()
-        for c in range(3):
-            for t in range(BLOCKS):
-                spread_copy(c, t).wait_send()
-            near_copy(c).wait_send()
+        combine(0, [first])
 
     @pl.when(sa == 1)
     def _():
-        write_basis(4, [other, sketch], lambda c: None)
-        drain(False)
-        for c in range(3):
-            for k in range(2):
-                relay_copy(c, far_first + k).wait_send()
+        combine(4, [first, second])
 
     for c in range(3):
         store(c).wait()
-    for first_sem, buffer, me, peer, count in levels:
-        for copy in sums(first_sem, buffer, me, peer, count):
-            copy.wait_send()
 
 
 def shards(forcing, velocity, wall_solve):
@@ -622,11 +683,16 @@
     edges = (4, 2, 3, BLOCKS, CELLS, 1, NY)
     vmem = pl.BlockSpec(memory_space=pltpu.VMEM)
     hbm = pl.BlockSpec(memory_space=pl.ANY)
-    return pl.pallas_call(
-        functools.partial(kernel, float(entries)),
-        out_shape=(jax.ShapeDtypeStruct(tile, f32), jax.ShapeDtypeStruct((8, 8), f32)),
+    array = jax.ShapeDtypeStruct(tile, f32)
+    low, high, gram = pl.pallas_call(
+        kernel,
+        out_shape=(
+            array,
+            array,
+            jax.ShapeDtypeStruct((8, 128), f32),
+        ),
         in_specs=[hbm, vmem, vmem],
-        out_specs=(hbm, vmem),
+        out_specs=(hbm, hbm, vmem),
         scratch_shapes=[
             pltpu.VMEM(padded, f32),
             pltpu.VMEM(padded, f32),
@@ -637,7 +703,8 @@
             pltpu.VMEM(tile, f32),
             pltpu.VMEM(edges, f32),
             pltpu.VMEM(edges, f32),
-            pltpu.VMEM((ROWS, 3 * NY), bf16),
+            pltpu.VMEM((HALF, 3 * NY), bf16),
+            pltpu.VMEM((HALF, 3 * NY), bf16),
             pltpu.VMEM((3 * NY, NY), bf16),
             pltpu.VMEM((3 * NY, NY), bf16),
             pltpu.VMEM((1, NY), f32),
@@ -645,10 +712,7 @@
             pltpu.VMEM((BLOCKS, 8, NY), f32),
             pltpu.VMEM((8, 128), f32),
             pltpu.VMEM((8, 8, 128), f32),
-            pltpu.VMEM((4, 8, 128), f32),
-            pltpu.VMEM((4, 8, 128), f32),
-            pltpu.VMEM((9, 8, 128), f32),
-            pltpu.VMEM((8, 8, 128), f32),
+            pltpu.VMEM((16, 8, 128), f32),
             pltpu.SemaphoreType.DMA((2,)),
             pltpu.SemaphoreType.DMA((2, 3)),
             pltpu.SemaphoreType.DMA((2, 3)),
@@ -659,15 +723,31 @@
             pltpu.SemaphoreType.DMA((3, 4)),
             pltpu.SemaphoreType.DMA((3,)),
             pltpu.SemaphoreType.DMA((3,)),
-            pltpu.SemaphoreType.DMA((13,)),
-            pltpu.SemaphoreType.DMA((13,)),
-            pltpu.SemaphoreType.DMA((3,)),
+            pltpu.SemaphoreType.DMA((22,)),
+            pltpu.SemaphoreType.DMA((22,)),
+            pltpu.SemaphoreType.DMA((6,)),
         ],
         compiler_params=pltpu.CompilerParams(
             collective_id=0, has_side_effects=True, vmem_limit_bytes=56 << 20
         ),
         name="sketch",
     )(forcing, velocity.reshape(1, NY), wall_solve)
+    return pl.pallas_call(
+        functools.partial(basis_kernel, float(entries)),
+        out_shape=(array, jax.ShapeDtypeStruct((8, 8), f32)),
+        in_specs=[hbm, hbm, vmem],
+        out_specs=(hbm, vmem),
+        scratch_shapes=[
+            pltpu.VMEM((9, 8, 128), f32),
+            pltpu.VMEM((8, 8, 128), f32),
+            pltpu.VMEM(tile, f32),
+            pltpu.VMEM(tile, f32),
+            pltpu.VMEM(tile, f32),
+            pltpu.SemaphoreType.DMA((9,)),
+        ],
+        compiler_params=pltpu.CompilerParams(vmem_limit_bytes=60 << 20),
+        name="basis",
+    )(low, high, gram)
 
 
 def solution(mesh):

time: 117 us -> 114 us (0.974)
  local copies, waits for them, and re-layouts: 4.35 us -> 0 us
  Pallas kernels: 111 us -> 113 us
    unnamed x4 -> x0, local copies, waits for them, and re-layouts: 4.35 us -> none
    pallas_call x1 -> x2, Pallas kernels: 111 us -> 113 us  [the longest x1 108 us: shards(): pl.pallas_call(kernel, out_shape=(array, array, jax.ShapeDtypeStruct((8,...]
where the time goes in v4:
time: 114 us; the launch traced here: 113 us
  Pallas kernels  113 us (99%)
    pallas_call x1, Pallas kernels, shards(): pl.pallas_call(kernel, out_shape=(array, array, jax.ShapeDtypeStruct((8,...  108 us
    pallas_call x1, Pallas kernels, shards(): pl.pallas_call(functools.partial(basis_kernel, float(entries)), out_shape...  4.52 us

profile of v4, /device:TPU:1, one launch (start us, length us, event | category | flops | bytes accessed | tf_op | source)
XLA Modules:
  0.0 113.5 jit_solution(3596271708735193218)
XLA Ops:
  0.6 108.3 %sketch.1 = (f32[3,4,32,8,256]{4,3,2,1,0:T(8,128)}, f32[3,4,32,8,256]{4,3,2,1,0:T(8,128)}, f32[8,128]{1,0:T(8,128)}) custom-call(f32[3,4,32,8,256]{4,3,2,1,0:T(8,128)} %forcing.1, f32[1,256]{1,0:T(1,128)} %bitcast.1, f32[256,256]{1,0:T(8,128)} %wall.1), custom_call_target="tpu_custom_call" | custom-call | tf_op jit(solution)/shard_map/sketch/pallas_call | solution.py:687
  109.0 4.5 %basis.1 = (f32[3,4,32,8,256]{4,3,2,1,0:T(8,128)}, f32[8,8]{1,0:T(8,128)}) custom-call(f32[3,4,32,8,256]{4,3,2,1,0:T(8,128)} %get-tuple-element.5.low, f32[3,4,32,8,256]{4,3,2,1,0:T(8,128)} %get-tuple-element.6.high, f32[8,128]{1,0:T(8,128)} %get-tuple-element.7.gram), custom_call_target="tpu_custom_call" | custom-call | tf_op jit(solution)/shard_map/basis/pallas_call | solution.py:735

commit v5 on v4

--- a/solution.py
+++ b/solution.py
@@ -390,7 +390,7 @@
             give(2)
         else:
             for stage in stages:
-                for g in range(2):
+                for g in (1, 0):
                     stage(g)
 
     def spread_copy(c, t):
@@ -484,22 +484,22 @@
         for c in range(3):
             store_own(c).start()
         own_pairs = [(i, j) for i in range(BLOCKS) for j in range(i, BLOCKS)]
-        accs = tuple(zero for _ in own_pairs)
-        for c in range(3):
-            accs = products(c, accs, own_pairs, [sketch])
-        tile = zero
-        for n, (i, j) in enumerate(own_pairs):
-            tile = tile + place(i + 4, j + 4, accs[n])
-        for b in range(BLOCKS):
-            square = squares[b]
-            tile = tile + place(b + 4, 8, square[:, :128] + square[:, 128:])
-        local_gram[...] = tile
         pairs = [(i, j) for i in range(BLOCKS) for j in range(i, 2 * BLOCKS)]
+        own_accs = tuple(zero for _ in own_pairs)
         accs = tuple(zero for _ in pairs)
         for c in range(3):
             for k in range(2):
                 sketch_wait(c, far_first + k)
                 relay_copy(c, far_first + k).start()
+            own_accs = products(c, own_accs, own_pairs, [sketch])
+            if c == 2:
+                tile = zero
+                for n, (i, j) in enumerate(own_pairs):
+                    tile = tile + place(i + 4, j + 4, own_accs[n])
+                for b in range(BLOCKS):
+                    square = squares[b]
+                    tile = tile + place(b + 4, 8, square[:, :128] + square[:, 128:])
+                local_gram[...] = tile
             for k in range(2):
                 sketch_wait(c, near_first + k)
             store(c).start()

time: 114 us -> 114 us (level)
  no operation moved by 1% of the time
where the time goes in v5:
time: 114 us; the launch traced here: 113 us
  Pallas kernels  113 us (99%)
    pallas_call x1, Pallas kernels, shards(): pl.pallas_call(kernel, out_shape=(array, array, jax.ShapeDtypeStruct((8,...  108 us
    pallas_call x1, Pallas kernels, shards(): pl.pallas_call(functools.partial(basis_kernel, float(entries)), out_shape...  4.52 us

profile of v5, /device:TPU:1, one launch (start us, length us, event | category | flops | bytes accessed | tf_op | source)
XLA Modules:
  0.0 113.5 jit_solution(8744910307551123093)
XLA Ops:
  0.6 108.3 %sketch.1 = (f32[3,4,32,8,256]{4,3,2,1,0:T(8,128)}, f32[3,4,32,8,256]{4,3,2,1,0:T(8,128)}, f32[8,128]{1,0:T(8,128)}) custom-call(f32[3,4,32,8,256]{4,3,2,1,0:T(8,128)} %forcing.1, f32[1,256]{1,0:T(1,128)} %bitcast.1, f32[256,256]{1,0:T(8,128)} %wall.1), custom_call_target="tpu_custom_call" | custom-call | tf_op jit(solution)/shard_map/sketch/pallas_call | solution.py:687
  109.0 4.5 %basis.1 = (f32[3,4,32,8,256]{4,3,2,1,0:T(8,128)}, f32[8,8]{1,0:T(8,128)}) custom-call(f32[3,4,32,8,256]{4,3,2,1,0:T(8,128)} %get-tuple-element.5.low, f32[3,4,32,8,256]{4,3,2,1,0:T(8,128)} %get-tuple-element.6.high, f32[8,128]{1,0:T(8,128)} %get-tuple-element.7.gram), custom_call_target="tpu_custom_call" | custom-call | tf_op jit(solution)/shard_map/basis/pallas_call | solution.py:735

commit v6 on v4

--- a/solution.py
+++ b/solution.py
@@ -14,7 +14,7 @@
 BLOCKS = 4
 CELLS = 32
 NY = 256
-HALF = 256
+PIECE = 128
 
 
 def kernel(
@@ -35,6 +35,8 @@
     edge_in,
     lhs0,
     lhs1,
+    lhs2,
+    lhs3,
     solve,
     solve_t,
     drift_row,
@@ -165,8 +167,8 @@
         flat = value.reshape(rows, NY)
         high = flat.astype(jnp.bfloat16)
         low = (flat - high.astype(jnp.float32)).astype(jnp.bfloat16)
-        target = (lhs0, lhs1)[start // HALF]
-        place = pl.ds(start % HALF, rows)
+        target = (lhs0, lhs1, lhs2, lhs3)[start // PIECE]
+        place = pl.ds(start % PIECE, rows)
         target[place, pl.ds(0, NY)] = high
         target[place, pl.ds(NY, NY)] = low
         target[place, pl.ds(2 * NY, NY)] = high
@@ -174,7 +176,7 @@
     def product(weights):
         return [
             jnp.dot(part[...], weights[...], preferred_element_type=jnp.float32)
-            for part in (lhs0, lhs1)
+            for part in (lhs0, lhs1, lhs2, lhs3)
         ]
 
     def halo_copy(e, g, field, merged, k):
@@ -295,7 +297,7 @@
             out = {}
             for i in range(nc):
                 for b in range(BLOCKS):
-                    half, first = divmod((i * BLOCKS + b) * tile, HALF)
+                    half, first = divmod((i * BLOCKS + b) * tile, PIECE)
                     out[i, b] = prod[half][first : first + tile].reshape(width, 8, NY)
             return out
 
@@ -703,8 +705,10 @@
             pltpu.VMEM(tile, f32),
             pltpu.VMEM(edges, f32),
             pltpu.VMEM(edges, f32),
-            pltpu.VMEM((HALF, 3 * NY), bf16),
-            pltpu.VMEM((HALF, 3 * NY), bf16),
+            pltpu.VMEM((PIECE, 3 * NY), bf16),
+            pltpu.VMEM((PIECE, 3 * NY), bf16),
+            pltpu.VMEM((PIECE, 3 * NY), bf16),
+            pltpu.VMEM((PIECE, 3 * NY), bf16),
             pltpu.VMEM((3 * NY, NY), bf16),
             pltpu.VMEM((3 * NY, NY), bf16),
             pltpu.VMEM((1, NY), f32),

time: 114 us -> 113 us (level)
  no operation moved by 1% of the time
where the time goes in v6:
time: 113 us
  Pallas kernels  113 us (100%)
    pallas_call x1, Pallas kernels, shards(): pl.pallas_call(kernel, out_shape=(array, array, jax.ShapeDtypeStruct((8,...  108 us
    pallas_call x1, Pallas kernels, shards(): pl.pallas_call(functools.partial(basis_kernel, float(entries)), out_shape...  4.52 us

profile of v6, /device:TPU:1, one launch (start us, length us, event | category | flops | bytes accessed | tf_op | source)
XLA Modules:
  0.0 113.2 jit_solution(11642455502591862491)
XLA Ops:
  0.6 108.1 %sketch.1 = (f32[3,4,32,8,256]{4,3,2,1,0:T(8,128)}, f32[3,4,32,8,256]{4,3,2,1,0:T(8,128)}, f32[8,128]{1,0:T(8,128)}) custom-call(f32[3,4,32,8,256]{4,3,2,1,0:T(8,128)} %forcing.1, f32[1,256]{1,0:T(1,128)} %bitcast.1, f32[256,256]{1,0:T(8,128)} %wall.1), custom_call_target="tpu_custom_call" | custom-call | tf_op jit(solution)/shard_map/sketch/pallas_call | solution.py:689
  108.7 4.5 %basis.1 = (f32[3,4,32,8,256]{4,3,2,1,0:T(8,128)}, f32[8,8]{1,0:T(8,128)}) custom-call(f32[3,4,32,8,256]{4,3,2,1,0:T(8,128)} %get-tuple-element.5.low, f32[3,4,32,8,256]{4,3,2,1,0:T(8,128)} %get-tuple-element.6.high, f32[8,128]{1,0:T(8,128)} %get-tuple-element.7.gram), custom_call_target="tpu_custom_call" | custom-call | tf_op jit(solution)/shard_map/basis/pallas_call | solution.py:739
